TPU v7x, 128 devices: a whole 4x4x4 slice. The times are simulated.
128 devices in a mesh: dp: 8 (over y, z_hi), ctx: 16 (over x, z_lo, core).
Axes of the slice: x: 4, y: 4, z: 4 (z_hi: 2, z_lo: 2; z = z_hi * 2 + z_lo), core: 2. Of those that a mesh axis runs over, the one named last changes fastest.
Arguments:
- inputs: bfloat16 [8, 2048, 4096], P('dp', 'ctx'), may hold values from -8 to 8
- queries: bfloat16 [8, 2048, 8192], P('dp', 'ctx'), may hold values from -256 to 256
- grad_output: bfloat16 [8, 2048, 8192], P('dp', 'ctx'), may hold values from -6 to 6
- kv_weight: bfloat16 [4096, 1024], P(('dp', 'ctx')), may hold values from -1 to 1
Outputs:
- attn_out: bfloat16 [8, 2048, 8192], P('dp', 'ctx')
- grad_query: bfloat16 [8, 2048, 8192], P('dp', 'ctx')
- grad_inputs: bfloat16 [8, 2048, 4096], P('dp', 'ctx')
- grad_weight: float32 [4096, 1024], P(('dp', 'ctx'))
All inputs are finite; a program needn't handle non-finite values.
Results may differ from a plain program's by a relative error of at most 0.035.
Values may be sent and summed in bfloat16 or wider, within the bound.
A program may use at most 128 MiB of HBM per device.

v0:
```python
import jax
import jax.numpy as jnp
from jax import lax
from jax.sharding import PartitionSpec as P

DH = 128


ROPE_BASE = 500000.0


def shifted(block, axis, distance):
    devices = range(lax.axis_size(axis))
    route = [(i - distance, i) for i in devices if i - distance in devices]
    return lax.ppermute(block, axis, route)


def shifted_2(value, axis, steps):
    count = lax.axis_size(axis)
    pairs = [(source, (source + steps) % count) for source in range(count)]
    return lax.ppermute(value, axis, pairs)


def rope_tables(positions, head_dim):
    half_dim = head_dim // 2
    frequency = ROPE_BASE ** (-2.0 * jnp.arange(half_dim, dtype=jnp.float32) / head_dim)
    angles = positions.astype(jnp.float32)[:, None] * frequency[None, :]
    return (jnp.cos(angles)[:, None, :], jnp.sin(angles)[:, None, :])


def rotary(values, positions):
    half_dim = values.shape[-1] // 2
    cosine, sine_table = rope_tables(positions, values.shape[-1])
    first_half = values[..., :half_dim]
    second = values[..., half_dim:]
    return jnp.concatenate(
        [first_half * cosine - second * sine_table, second * cosine + first_half * sine_table],
        axis=-1,
    )


def rotary_back(gradient, positions):
    half_dim = gradient.shape[-1] // 2
    cosine, sine_table = rope_tables(positions, gradient.shape[-1])
    first_half = gradient[..., :half_dim]
    second = gradient[..., half_dim:]
    return jnp.concatenate(
        [first_half * cosine + second * sine_table, second * cosine - first_half * sine_table],
        axis=-1,
    )


def on_device(inputs, queries, grad_output, kv_weight):
    token_count = inputs.shape[1]
    kv_width = kv_weight.shape[1]
    kv_half = kv_width // 2
    head_dim = DH
    kv_heads = kv_half // head_dim
    q_heads = queries.shape[2] // head_dim
    group_size = q_heads // kv_heads
    row_count = group_size * token_count
    ctx_size = lax.axis_size("ctx")
    ctx_index = lax.axis_index("ctx")
    score_scale = head_dim ** (-0.5)
    tokens = inputs[0]
    weight_all = lax.all_gather(kv_weight, ("dp", "ctx"), axis=0, tiled=True)
    projected = jnp.dot(tokens, weight_all, preferred_element_type=jnp.float32)
    positions = ctx_index * token_count + jnp.arange(token_count, dtype=jnp.int32)
    key_rows = rotary(
        projected[:, :kv_half].reshape(token_count, kv_heads, head_dim), positions
    ).astype(jnp.bfloat16)
    value_rows = projected[:, kv_half:].astype(jnp.bfloat16)
    own_block = jnp.concatenate([key_rows.reshape(token_count, kv_half), value_rows], axis=1)

    def head_rows(matrix):
        return (
            matrix.reshape(token_count, kv_heads, group_size, head_dim)
            .transpose(1, 2, 0, 3)
            .reshape(kv_heads, row_count, head_dim)
        )

    def token_rows(rows_by_head):
        return (
            rows_by_head.reshape(kv_heads, group_size, token_count, head_dim)
            .transpose(2, 0, 1, 3)
            .reshape(token_count, q_heads * head_dim)
        )

    query_rows = head_rows(queries[0])
    grad_rows = head_rows(grad_output[0])
    query_pos = jnp.arange(row_count, dtype=jnp.int32) % token_count
    key_pos = jnp.arange(token_count, dtype=jnp.int32)

    def split_block(kv_block):
        key_part = kv_block[:, :kv_half].reshape(token_count, kv_heads, head_dim)
        value_part = kv_block[:, kv_half:].reshape(token_count, kv_heads, head_dim)
        return (key_part, value_part)

    def block_scores(key_part, block_id):
        scores = (
            jnp.einsum("hrd,khd->hrk", query_rows, key_part, preferred_element_type=jnp.float32)
            * score_scale
        )
        allowed = (block_id < ctx_index) | (query_pos[:, None] >= key_pos[None, :])
        return (scores, allowed)

    def forward_update(state_now, kv_block, block_id):
        row_top, row_total, row_accum = state_now
        key_part, value_part = split_block(kv_block)
        scores, allowed = block_scores(key_part, block_id)
        scores = jnp.where(allowed[None], scores, -jnp.inf)
        new_top = jnp.maximum(row_top, jnp.max(scores, axis=-1, keepdims=True))
        weights = jnp.exp(scores - new_top)
        factor = jnp.exp(row_top - new_top)
        row_total = row_total * factor + jnp.sum(weights, axis=-1, keepdims=True)
        row_accum = row_accum * factor + jnp.einsum(
            "hrk,khd->hrd",
            weights.astype(jnp.bfloat16),
            value_part,
            preferred_element_type=jnp.float32,
        )
        return (new_top, row_total, row_accum)

    start_state = (
        jnp.full((kv_heads, row_count, 1), -jnp.inf, jnp.float32),
        jnp.zeros((kv_heads, row_count, 1), jnp.float32),
        jnp.zeros((kv_heads, row_count, head_dim), jnp.float32),
    )
    state_now = forward_update(start_state, own_block, ctx_index)
    kv_store = jnp.zeros((ctx_size, token_count, kv_width), jnp.bfloat16)
    kv_store = lax.dynamic_update_slice_in_dim(kv_store, own_block[None], ctx_index, 0)

    def forward_step(offset, loop_state):
        kv_block, stored_now, state_here = loop_state
        kv_block = shifted(kv_block, "ctx", 1)
        source = ctx_index - offset

        def take_block(operands):
            stored, current = operands
            stored = lax.dynamic_update_slice_in_dim(stored, kv_block[None], source, 0)
            return (stored, forward_update(current, kv_block, source))

        def keep_state(operands):
            return operands

        stored_now, state_here = lax.cond(
            offset <= ctx_index, take_block, keep_state, (stored_now, state_here)
        )
        return (kv_block, stored_now, state_here)

    last_block, kv_store, state_now = lax.fori_loop(
        1, ctx_size, forward_step, (own_block, kv_store, state_now)
    )
    row_top, row_total, row_accum = state_now
    attn_rows = (row_accum / row_total).astype(jnp.bfloat16)
    log_total = row_top + jnp.log(row_total)
    row_delta = jnp.sum(
        grad_rows.astype(jnp.float32) * attn_rows.astype(jnp.float32), axis=-1, keepdims=True
    )
    attn_out = token_rows(attn_rows)[None]

    def backward_terms(kv_block, block_id):
        key_part, value_part = split_block(kv_block)
        scores, allowed = block_scores(key_part, block_id)
        probs_now = jnp.where(allowed[None], jnp.exp(scores - log_total), 0.0)
        dprobs = jnp.einsum(
            "hrd,khd->hrk", grad_rows, value_part, preferred_element_type=jnp.float32
        )
        dscores = (probs_now * (dprobs - row_delta)).astype(jnp.bfloat16)
        grad_keys = (
            jnp.einsum("hrk,hrd->khd", dscores, query_rows, preferred_element_type=jnp.float32)
            * score_scale
        )
        grad_values = jnp.einsum(
            "hrk,hrd->khd",
            probs_now.astype(jnp.bfloat16),
            grad_rows,
            preferred_element_type=jnp.float32,
        )
        query_part = jnp.einsum(
            "hrk,khd->hrd", dscores, key_part, preferred_element_type=jnp.float32
        )
        block_grads = jnp.concatenate(
            [grad_keys.reshape(token_count, kv_half), grad_values.reshape(token_count, kv_half)],
            axis=1,
        )
        return (block_grads, query_part)

    def add_block(operands, block_id):
        grad_block, grad_query_sum = operands
        kv_block = lax.dynamic_slice_in_dim(kv_store, block_id, 1, 0)[0]
        block_grads, query_part = backward_terms(kv_block, block_id)
        return (grad_block + block_grads, grad_query_sum + query_part)

    def skip_block(operand_pair):
        return operand_pair

    zero_grads = jnp.zeros((token_count, kv_width), jnp.float32)
    zero_query = jnp.zeros((kv_heads, row_count, head_dim), jnp.float32)

    def backward_step(offset, operands):
        source = ctx_index - offset

        def include(operand_pair):
            return add_block(operand_pair, source)

        grad_block, grad_query_sum = lax.cond(offset <= ctx_index, include, skip_block, operands)
        grad_block = shifted_2(grad_block.astype(jnp.bfloat16), "ctx", 1).astype(grad_block.dtype)
        return (grad_block, grad_query_sum)

    grad_block, grad_query_sum = lax.fori_loop(0, ctx_size, backward_step, (zero_grads, zero_query))
    grad_query = token_rows(grad_query_sum * score_scale).astype(jnp.bfloat16)[None]
    grad_key_rows = rotary_back(
        grad_block[:, :kv_half].reshape(token_count, kv_heads, head_dim), positions
    ).reshape(token_count, kv_half)
    grad_projected = jnp.concatenate([grad_key_rows, grad_block[:, kv_half:]], axis=1).astype(
        jnp.bfloat16
    )
    grad_inputs = lax.dot_general(
        grad_projected, weight_all, (((1,), (1,)), ((), ())), preferred_element_type=jnp.float32
    ).astype(jnp.bfloat16)[None]
    grad_weight = lax.psum_scatter(
        lax.dot_general(
            tokens, grad_projected, (((0,), (0,)), ((), ())), preferred_element_type=jnp.float32
        ),
        ("dp", "ctx"),
        scatter_dimension=0,
        tiled=True,
    )
    return (attn_out, grad_query, grad_inputs, grad_weight)


def solution(mesh):
    in_specs = (
        P("dp", "ctx", None),
        P("dp", "ctx", None),
        P("dp", "ctx", None),
        P(("dp", "ctx"), None),
    )
    out_specs = (
        P("dp", "ctx", None),
        P("dp", "ctx", None),
        P("dp", "ctx", None),
        P(("dp", "ctx"), None),
    )
    return jax.shard_map(
        on_device, mesh=mesh, in_specs=in_specs, out_specs=out_specs, check_vma=False
    )
```

profile of v0, /device:TPU:0, one launch (start us, length us, event | category | flops | bytes accessed | tf_op | source)
XLA Modules:
  0.0 1567.8 jit_solution(14216864717612839760)
XLA Ops:
  8.0 2.2 copy.106
  10.2 3.8 copy.71
  14.0 2.8 reshape.234
  16.8 2.5 copy.76
  19.3 3.5 copy.108
  22.9 5.1 copy.79
  28.0 4.2 reshape.237
  33.4 182.2 %all-gather.2.cloned.1.call-done = bf16[4096,1024]{1,0:T(8,128)(2,1)} async-done(((bf16[32,1024]{1,0:T(8,128)(2,1)}), bf16[4096,1024]{1,0:T(8,128)(2,1)}) %all-gather.2.cloned.1.call-update) | async-done | bytes 8388624 | tf_op jit(solution)/shard_map/all_gather | solution.py:66
  215.6 4.6 fusion.28
  228.6 2.2 fusion.42
  231.5 3.3 convolution_add_fusion.1
  235.7 2.0 copy-done.6
  237.7 180.0 %while.38 = (s32[]{:T(128)}, bf16[128,1024]{0,1:T(8,128)(2,1)}, bf16[16,128,1024]{1,2,0:T(8,128)(2,1)}, f32[4,2048,1]{1,0,2:T(4,128)S(1)}, f32[4,2048,1]{1,0,2:T...) while((s32[]{:T(128)}, bf16[128,1024]{0,1:T(8,128)(2,1)}, ...), condition=%wide.region_7.8_spmd.clone, body=%wide.region_2.7_spmd.clone.sunk | while | flops 551063552 | bytes 61154760 | solution.py:151
  241.1 15.3 collective-permute-start
  258.4 6.5 collective-permute-start
  267.0 16.2 %collective-permute-start = (bf16[128,1024]{0,1:T(8,128)(2,1)}, bf16[128,1024]{0,1:T(8,128)(2,1)S(1)}, u32[]{:S(2)}, u32[]{:S(2)}) collective-permute-start(bf16[128,1024]{0,1:T(8,128)(2,1)} %get-tuple-element.838), channel_id=1, source_target_pairs={{0,1},{1,2},{2,3},{3,4},{4,5},{5,6},{6,7},{7,8},{8,9},{9,10},{10,1... | collective-permute-start | bytes 786440 | tf_op jit(solution)/shard_map/while/body/eval_jaxpr/ppermute | solution.py:15
  285.3 6.5 collective-permute-start
  293.9 12.5 collective-permute-start
  308.4 7.5 collective-permute-start
  318.0 17.1 %collective-permute-start = (bf16[128,1024]{0,1:T(8,128)(2,1)}, bf16[128,1024]{0,1:T(8,128)(2,1)S(1)}, u32[]{:S(2)}, u32[]{:S(2)}) collective-permute-start(bf16[128,1024]{0,1:T(8,128)(2,1)} %get-tuple-element.838), channel_id=1, source_target_pairs={{0,1},{1,2},{2,3},{3,4},{4,5},{5,6},{6,7},{7,8},{8,9},{9,10},{10,1... | collective-permute-start | bytes 786440 | tf_op jit(solution)/shard_map/while/body/eval_jaxpr/ppermute | solution.py:15
  337.1 7.4 collective-permute-start
  346.6 7.4 collective-permute-start
  356.1 7.4 collective-permute-start
  365.6 13.7 collective-permute-start
  381.3 7.4 collective-permute-start
  390.8 15.3 collective-permute-start
  408.2 7.4 collective-permute-start
  417.7 5.4 copy.77
  423.1 5.0 multiply_reduce_fusion
  428.1 2.2 broadcast.182
  430.3 439.3 %while.39 = (s32[]{:T(128)}, f32[128,1024]{0,1:T(8,128)}, f32[4,2048,128]{2,1,0:T(8,128)}, s32[]{:T(128)}, bf16[16,128,1024]{1,2,0:T(8,128)(2,1)}, /*index=5*/bf...) while((s32[]{:T(128)}, f32[128,1024]{0,1:T(8,128)}, ...), condition=%wide.region_12.13_spmd.clone, body=%wide.region_9.12_spmd.clone.sunk | while | flops 1351823360 | bytes 85468640 | solution.py:211
  431.1 11.4 conditional.7
  436.2 2.2 maximum_add_fusion
  438.4 2.2 convolution_add_fusion
  440.6 1.9 copy-done.5
  443.6 15.2 collective-permute-start.1
  458.9 85.0 %collective-permute-done.1 = bf16[128,1024]{0,1:T(8,128)(2,1)} collective-permute-done((bf16[128,1024]{0,1:T(8,128)(2,1)S(1)}, bf16[128,1024]{0,1:T(8,128)(2,1)}, u32[]{:S(2)}, u32[]{:S(2)}) %collective-permute-start.1) | collective-permute-done | bytes 262176 | tf_op jit(solution)/shard_map/while/body/eval_jaxpr/ppermute | solution.py:21
  545.7 1.9 broadcast_select_fusion.2
  548.7 14.7 collective-permute-done.1
  565.3 1.9 broadcast_select_fusion.2
  568.3 14.7 collective-permute-done.1
  587.9 14.7 collective-permute-done.1
  607.5 16.2 %collective-permute-done.1 = bf16[128,1024]{0,1:T(8,128)(2,1)} collective-permute-done((bf16[128,1024]{0,1:T(8,128)(2,1)S(1)}, bf16[128,1024]{0,1:T(8,128)(2,1)}, u32[]{:S(2)}, u32[]{:S(2)}) %collective-permute-start.1) | collective-permute-done | bytes 262176 | tf_op jit(solution)/shard_map/while/body/eval_jaxpr/ppermute | solution.py:21
  628.6 17.3 %collective-permute-done.1 = bf16[128,1024]{0,1:T(8,128)(2,1)} collective-permute-done((bf16[128,1024]{0,1:T(8,128)(2,1)S(1)}, bf16[128,1024]{0,1:T(8,128)(2,1)}, u32[]{:S(2)}, u32[]{:S(2)}) %collective-permute-start.1) | collective-permute-done | bytes 262176 | tf_op jit(solution)/shard_map/while/body/eval_jaxpr/ppermute | solution.py:21
  650.8 17.3 %collective-permute-done.1 = bf16[128,1024]{0,1:T(8,128)(2,1)} collective-permute-done((bf16[128,1024]{0,1:T(8,128)(2,1)S(1)}, bf16[128,1024]{0,1:T(8,128)(2,1)}, u32[]{:S(2)}, u32[]{:S(2)}) %collective-permute-start.1) | collective-permute-done | bytes 262176 | tf_op jit(solution)/shard_map/while/body/eval_jaxpr/ppermute | solution.py:21
  673.0 17.3 %collective-permute-done.1 = bf16[128,1024]{0,1:T(8,128)(2,1)} collective-permute-done((bf16[128,1024]{0,1:T(8,128)(2,1)S(1)}, bf16[128,1024]{0,1:T(8,128)(2,1)}, u32[]{:S(2)}, u32[]{:S(2)}) %collective-permute-start.1) | collective-permute-done | bytes 262176 | tf_op jit(solution)/shard_map/while/body/eval_jaxpr/ppermute | solution.py:21
  695.2 17.3 %collective-permute-done.1 = bf16[128,1024]{0,1:T(8,128)(2,1)} collective-permute-done((bf16[128,1024]{0,1:T(8,128)(2,1)S(1)}, bf16[128,1024]{0,1:T(8,128)(2,1)}, u32[]{:S(2)}, u32[]{:S(2)}) %collective-permute-start.1) | collective-permute-done | bytes 262176 | tf_op jit(solution)/shard_map/while/body/eval_jaxpr/ppermute | solution.py:21
  717.4 17.3 %collective-permute-done.1 = bf16[128,1024]{0,1:T(8,128)(2,1)} collective-permute-done((bf16[128,1024]{0,1:T(8,128)(2,1)S(1)}, bf16[128,1024]{0,1:T(8,128)(2,1)}, u32[]{:S(2)}, u32[]{:S(2)}) %collective-permute-start.1) | collective-permute-done | bytes 262176 | tf_op jit(solution)/shard_map/while/body/eval_jaxpr/ppermute | solution.py:21
  739.6 17.3 %collective-permute-done.1 = bf16[128,1024]{0,1:T(8,128)(2,1)} collective-permute-done((bf16[128,1024]{0,1:T(8,128)(2,1)S(1)}, bf16[128,1024]{0,1:T(8,128)(2,1)}, u32[]{:S(2)}, u32[]{:S(2)}) %collective-permute-start.1) | collective-permute-done | bytes 262176 | tf_op jit(solution)/shard_map/while/body/eval_jaxpr/ppermute | solution.py:21
  761.7 17.3 %collective-permute-done.1 = bf16[128,1024]{0,1:T(8,128)(2,1)} collective-permute-done((bf16[128,1024]{0,1:T(8,128)(2,1)S(1)}, bf16[128,1024]{0,1:T(8,128)(2,1)}, u32[]{:S(2)}, u32[]{:S(2)}) %collective-permute-start.1) | collective-permute-done | bytes 262176 | tf_op jit(solution)/shard_map/while/body/eval_jaxpr/ppermute | solution.py:21
  783.9 17.3 %collective-permute-done.1 = bf16[128,1024]{0,1:T(8,128)(2,1)} collective-permute-done((bf16[128,1024]{0,1:T(8,128)(2,1)S(1)}, bf16[128,1024]{0,1:T(8,128)(2,1)}, u32[]{:S(2)}, u32[]{:S(2)}) %collective-permute-start.1) | collective-permute-done | bytes 262176 | tf_op jit(solution)/shard_map/while/body/eval_jaxpr/ppermute | solution.py:21
  806.1 17.3 %collective-permute-done.1 = bf16[128,1024]{0,1:T(8,128)(2,1)} collective-permute-done((bf16[128,1024]{0,1:T(8,128)(2,1)S(1)}, bf16[128,1024]{0,1:T(8,128)(2,1)}, u32[]{:S(2)}, u32[]{:S(2)}) %collective-permute-start.1) | collective-permute-done | bytes 262176 | tf_op jit(solution)/shard_map/while/body/eval_jaxpr/ppermute | solution.py:21
  828.3 17.3 %collective-permute-done.1 = bf16[128,1024]{0,1:T(8,128)(2,1)} collective-permute-done((bf16[128,1024]{0,1:T(8,128)(2,1)S(1)}, bf16[128,1024]{0,1:T(8,128)(2,1)}, u32[]{:S(2)}, u32[]{:S(2)}) %collective-permute-start.1) | collective-permute-done | bytes 262176 | tf_op jit(solution)/shard_map/while/body/eval_jaxpr/ppermute | solution.py:21
  850.5 17.3 %collective-permute-done.1 = bf16[128,1024]{0,1:T(8,128)(2,1)} collective-permute-done((bf16[128,1024]{0,1:T(8,128)(2,1)S(1)}, bf16[128,1024]{0,1:T(8,128)(2,1)}, u32[]{:S(2)}, u32[]{:S(2)}) %collective-permute-start.1) | collective-permute-done | bytes 262176 | tf_op jit(solution)/shard_map/while/body/eval_jaxpr/ppermute | solution.py:21
  873.1 8.1 convolution_bitcast_fusion
  881.2 17.4 %copy.98 = f32[4096,1024]{1,0:T(8,128)} copy(f32[4096,1024]{0,1:T(8,128)} %convolution_bitcast_fusion) | data formatting | bytes 33554432
  898.6 2.2 copy.107
  900.8 3.8 copy.78
  904.6 4.2 broadcast_in_dim_reshape.3
  908.8 2.6 multiply_convert_fusion
  911.4 2.7 copy.119
  914.1 4.2 convert_element_type.98
  918.2 7.2 fusion.22
  925.5 635.5 %reduce-scatter.4.cloned.1.call-done = f32[32,1024]{1,0:T(8,128)} async-done(((f32[4096,1024]{1,0:T(8,128)}), f32[32,1024]{1,0:T(8,128)}) %reduce-scatter.4.cloned.1.call-update) | async-done | bytes 131088
  (274 shorter events, 125.0 us)
Async XLA Ops:
  7.2 208.4 %copy-start = (bf16[1,128,4096]{2,1,0:T(8,128)(2,1)S(1)}, bf16[1,128,4096]{2,1,0:T(8,128)(2,1)}, u32[]{:S(2)}) copy-start(bf16[1,128,4096]{2,1,0:T(8,128)(2,1)} %param.12) | copy-start | bytes 3145732
  7.2 208.4 %all-gather.2.cloned.1.call-start = ((), (), s32[]{:S(2)}) async-start(), calls=%async_computation.1 | async-start | bytes 8454144 | tf_op jit(solution)/shard_map/all_gather | solution.py:66
  7.9 1553.0 %reduce-scatter.4.cloned.1.call-start = ((), (), s32[]{:S(2)}) async-start(), calls=%async_computation.2 | async-start | bytes 16908288
  32.5 190.6 %copy-start.10 = (f32[128,64]{1,0:T(8,128)}, f32[128,64]{1,0:T(8,128)S(1)}, u32[]{:S(2)}) copy-start(f32[128,64]{1,0:T(8,128)S(1)} %get-tuple-element.695) | copy-start | bytes 98308
  32.5 190.5 %copy-start.11 = (f32[128,64]{1,0:T(8,128)}, f32[128,64]{1,0:T(8,128)S(1)}, u32[]{:S(2)}) copy-start(f32[128,64]{1,0:T(8,128)S(1)} %get-tuple-element.696) | copy-start | bytes 98308
  220.2 0.8 copy-start.7
  228.6 2.9 copy-start.8
  234.7 0.9 copy-start.9
  235.7 2.0 copy-start.6
  237.7 2.7 collective-permute-start
  241.1 16.7 %collective-permute-start = (bf16[128,1024]{0,1:T(8,128)(2,1)}, bf16[128,1024]{0,1:T(8,128)(2,1)S(1)}, u32[]{:S(2)}, u32[]{:S(2)}) collective-permute-start(bf16[128,1024]{0,1:T(8,128)(2,1)} %get-tuple-element.838), channel_id=1, source_target_pairs={{0,1},{1,2},{2,3},{3,4},{4,5},{5,6},{6,7},{7,8},{8,9},{9,10},{10,1... | collective-permute-start | bytes 786440 | tf_op jit(solution)/shard_map/while/body/eval_jaxpr/ppermute | solution.py:15
  258.4 7.9 collective-permute-start
  267.0 17.5 %collective-permute-start = (bf16[128,1024]{0,1:T(8,128)(2,1)}, bf16[128,1024]{0,1:T(8,128)(2,1)S(1)}, u32[]{:S(2)}, u32[]{:S(2)}) collective-permute-start(bf16[128,1024]{0,1:T(8,128)(2,1)} %get-tuple-element.838), channel_id=1, source_target_pairs={{0,1},{1,2},{2,3},{3,4},{4,5},{5,6},{6,7},{7,8},{8,9},{9,10},{10,1... | collective-permute-start | bytes 786440 | tf_op jit(solution)/shard_map/while/body/eval_jaxpr/ppermute | solution.py:15
  285.3 7.9 collective-permute-start
  293.9 13.9 collective-permute-start
  308.4 8.8 collective-permute-start
  318.0 18.4 %collective-permute-start = (bf16[128,1024]{0,1:T(8,128)(2,1)}, bf16[128,1024]{0,1:T(8,128)(2,1)S(1)}, u32[]{:S(2)}, u32[]{:S(2)}) collective-permute-start(bf16[128,1024]{0,1:T(8,128)(2,1)} %get-tuple-element.838), channel_id=1, source_target_pairs={{0,1},{1,2},{2,3},{3,4},{4,5},{5,6},{6,7},{7,8},{8,9},{9,10},{10,1... | collective-permute-start | bytes 786440 | tf_op jit(solution)/shard_map/while/body/eval_jaxpr/ppermute | solution.py:15
  337.1 8.8 collective-permute-start
  346.6 8.8 collective-permute-start
  356.1 8.8 collective-permute-start
  365.6 15.0 collective-permute-start
  381.3 8.8 collective-permute-start
  390.8 16.7 %collective-permute-start = (bf16[128,1024]{0,1:T(8,128)(2,1)}, bf16[128,1024]{0,1:T(8,128)(2,1)S(1)}, u32[]{:S(2)}, u32[]{:S(2)}) collective-permute-start(bf16[128,1024]{0,1:T(8,128)(2,1)} %get-tuple-element.838), channel_id=1, source_target_pairs={{0,1},{1,2},{2,3},{3,4},{4,5},{5,6},{6,7},{7,8},{8,9},{9,10},{10,1... | collective-permute-start | bytes 786440 | tf_op jit(solution)/shard_map/while/body/eval_jaxpr/ppermute | solution.py:15
  408.2 8.8 collective-permute-start
  431.1 2.8 copy-start.1
  435.4 3.0 copy-start.4
  440.6 1.9 copy-start.5
  443.6 100.2 %collective-permute-start.1 = (bf16[128,1024]{0,1:T(8,128)(2,1)S(1)}, bf16[128,1024]{0,1:T(8,128)(2,1)}, u32[]{:S(2)}, u32[]{:S(2)}) collective-permute-start(bf16[128,1024]{0,1:T(8,128)(2,1)S(1)} %convert_element_type.130), channel_id=1, source_target_pairs={{0,1},{1,2},{2,3},{3,4},{4,5},{5,6},{6,7},{7,8},{8,9},{9,10},{10,1... | collective-permute-start | bytes 786440 | tf_op jit(solution)/shard_map/while/body/eval_jaxpr/ppermute | solution.py:21
  548.6 14.8 collective-permute-start.1
  568.2 14.8 collective-permute-start.1
  587.8 14.8 collective-permute-start.1
  607.4 16.3 %collective-permute-start.1 = (bf16[128,1024]{0,1:T(8,128)(2,1)S(1)}, bf16[128,1024]{0,1:T(8,128)(2,1)}, u32[]{:S(2)}, u32[]{:S(2)}) collective-permute-start(bf16[128,1024]{0,1:T(8,128)(2,1)S(1)} %convert_element_type.130), channel_id=1, source_target_pairs={{0,1},{1,2},{2,3},{3,4},{4,5},{5,6},{6,7},{7,8},{8,9},{9,10},{10,1... | collective-permute-start | bytes 786440 | tf_op jit(solution)/shard_map/while/body/eval_jaxpr/ppermute | solution.py:21
  628.5 17.4 %collective-permute-start.1 = (bf16[128,1024]{0,1:T(8,128)(2,1)S(1)}, bf16[128,1024]{0,1:T(8,128)(2,1)}, u32[]{:S(2)}, u32[]{:S(2)}) collective-permute-start(bf16[128,1024]{0,1:T(8,128)(2,1)S(1)} %convert_element_type.130), channel_id=1, source_target_pairs={{0,1},{1,2},{2,3},{3,4},{4,5},{5,6},{6,7},{7,8},{8,9},{9,10},{10,1... | collective-permute-start | bytes 786440 | tf_op jit(solution)/shard_map/while/body/eval_jaxpr/ppermute | solution.py:21
  650.7 17.4 %collective-permute-start.1 = (bf16[128,1024]{0,1:T(8,128)(2,1)S(1)}, bf16[128,1024]{0,1:T(8,128)(2,1)}, u32[]{:S(2)}, u32[]{:S(2)}) collective-permute-start(bf16[128,1024]{0,1:T(8,128)(2,1)S(1)} %convert_element_type.130), channel_id=1, source_target_pairs={{0,1},{1,2},{2,3},{3,4},{4,5},{5,6},{6,7},{7,8},{8,9},{9,10},{10,1... | collective-permute-start | bytes 786440 | tf_op jit(solution)/shard_map/while/body/eval_jaxpr/ppermute | solution.py:21
  672.9 17.4 %collective-permute-start.1 = (bf16[128,1024]{0,1:T(8,128)(2,1)S(1)}, bf16[128,1024]{0,1:T(8,128)(2,1)}, u32[]{:S(2)}, u32[]{:S(2)}) collective-permute-start(bf16[128,1024]{0,1:T(8,128)(2,1)S(1)} %convert_element_type.130), channel_id=1, source_target_pairs={{0,1},{1,2},{2,3},{3,4},{4,5},{5,6},{6,7},{7,8},{8,9},{9,10},{10,1... | collective-permute-start | bytes 786440 | tf_op jit(solution)/shard_map/while/body/eval_jaxpr/ppermute | solution.py:21
  695.1 17.4 %collective-permute-start.1 = (bf16[128,1024]{0,1:T(8,128)(2,1)S(1)}, bf16[128,1024]{0,1:T(8,128)(2,1)}, u32[]{:S(2)}, u32[]{:S(2)}) collective-permute-start(bf16[128,1024]{0,1:T(8,128)(2,1)S(1)} %convert_element_type.130), channel_id=1, source_target_pairs={{0,1},{1,2},{2,3},{3,4},{4,5},{5,6},{6,7},{7,8},{8,9},{9,10},{10,1... | collective-permute-start | bytes 786440 | tf_op jit(solution)/shard_map/while/body/eval_jaxpr/ppermute | solution.py:21
  717.3 17.4 %collective-permute-start.1 = (bf16[128,1024]{0,1:T(8,128)(2,1)S(1)}, bf16[128,1024]{0,1:T(8,128)(2,1)}, u32[]{:S(2)}, u32[]{:S(2)}) collective-permute-start(bf16[128,1024]{0,1:T(8,128)(2,1)S(1)} %convert_element_type.130), channel_id=1, source_target_pairs={{0,1},{1,2},{2,3},{3,4},{4,5},{5,6},{6,7},{7,8},{8,9},{9,10},{10,1... | collective-permute-start | bytes 786440 | tf_op jit(solution)/shard_map/while/body/eval_jaxpr/ppermute | solution.py:21
  739.5 17.4 %collective-permute-start.1 = (bf16[128,1024]{0,1:T(8,128)(2,1)S(1)}, bf16[128,1024]{0,1:T(8,128)(2,1)}, u32[]{:S(2)}, u32[]{:S(2)}) collective-permute-start(bf16[128,1024]{0,1:T(8,128)(2,1)S(1)} %convert_element_type.130), channel_id=1, source_target_pairs={{0,1},{1,2},{2,3},{3,4},{4,5},{5,6},{6,7},{7,8},{8,9},{9,10},{10,1... | collective-permute-start | bytes 786440 | tf_op jit(solution)/shard_map/while/body/eval_jaxpr/ppermute | solution.py:21
  761.7 17.4 %collective-permute-start.1 = (bf16[128,1024]{0,1:T(8,128)(2,1)S(1)}, bf16[128,1024]{0,1:T(8,128)(2,1)}, u32[]{:S(2)}, u32[]{:S(2)}) collective-permute-start(bf16[128,1024]{0,1:T(8,128)(2,1)S(1)} %convert_element_type.130), channel_id=1, source_target_pairs={{0,1},{1,2},{2,3},{3,4},{4,5},{5,6},{6,7},{7,8},{8,9},{9,10},{10,1... | collective-permute-start | bytes 786440 | tf_op jit(solution)/shard_map/while/body/eval_jaxpr/ppermute | solution.py:21
  783.9 17.4 %collective-permute-start.1 = (bf16[128,1024]{0,1:T(8,128)(2,1)S(1)}, bf16[128,1024]{0,1:T(8,128)(2,1)}, u32[]{:S(2)}, u32[]{:S(2)}) collective-permute-start(bf16[128,1024]{0,1:T(8,128)(2,1)S(1)} %convert_element_type.130), channel_id=1, source_target_pairs={{0,1},{1,2},{2,3},{3,4},{4,5},{5,6},{6,7},{7,8},{8,9},{9,10},{10,1... | collective-permute-start | bytes 786440 | tf_op jit(solution)/shard_map/while/body/eval_jaxpr/ppermute | solution.py:21
  806.0 17.4 %collective-permute-start.1 = (bf16[128,1024]{0,1:T(8,128)(2,1)S(1)}, bf16[128,1024]{0,1:T(8,128)(2,1)}, u32[]{:S(2)}, u32[]{:S(2)}) collective-permute-start(bf16[128,1024]{0,1:T(8,128)(2,1)S(1)} %convert_element_type.130), channel_id=1, source_target_pairs={{0,1},{1,2},{2,3},{3,4},{4,5},{5,6},{6,7},{7,8},{8,9},{9,10},{10,1... | collective-permute-start | bytes 786440 | tf_op jit(solution)/shard_map/while/body/eval_jaxpr/ppermute | solution.py:21
  828.2 17.4 %collective-permute-start.1 = (bf16[128,1024]{0,1:T(8,128)(2,1)S(1)}, bf16[128,1024]{0,1:T(8,128)(2,1)}, u32[]{:S(2)}, u32[]{:S(2)}) collective-permute-start(bf16[128,1024]{0,1:T(8,128)(2,1)S(1)} %convert_element_type.130), channel_id=1, source_target_pairs={{0,1},{1,2},{2,3},{3,4},{4,5},{5,6},{6,7},{7,8},{8,9},{9,10},{10,1... | collective-permute-start | bytes 786440 | tf_op jit(solution)/shard_map/while/body/eval_jaxpr/ppermute | solution.py:21
  850.4 17.4 %collective-permute-start.1 = (bf16[128,1024]{0,1:T(8,128)(2,1)S(1)}, bf16[128,1024]{0,1:T(8,128)(2,1)}, u32[]{:S(2)}, u32[]{:S(2)}) collective-permute-start(bf16[128,1024]{0,1:T(8,128)(2,1)S(1)} %convert_element_type.130), channel_id=1, source_target_pairs={{0,1},{1,2},{2,3},{3,4},{4,5},{5,6},{6,7},{7,8},{8,9},{9,10},{10,1... | collective-permute-start | bytes 786440 | tf_op jit(solution)/shard_map/while/body/eval_jaxpr/ppermute | solution.py:21
Sparse Core Ops, SparseCore 0:
  9.7 205.8 all-gather.1
  898.7 662.1 reduce-scatter.3
where the time goes:
time: 1570 us
  waiting for transfers between devices  1170 us (75%)
  starting transfers between devices  166 us (11%)
  local copies, waits for them, and re-layouts  91.6 us (6%)
  other arithmetic  90.5 us (6%)
  matrix products  31.1 us (2%)
    unnamed x3, waiting for transfers between devices  636 us
    ppermute x16, waiting for transfers between devices, shifted_2(): return lax.ppermute(value, axis, pairs)  336 us
    all_gather x1, waiting for transfers between devices, on_device(): weight_all = lax.all_gather(kv_weight, ('dp', 'ctx'), axis=0, tiled=True)  182 us
    ppermute x15, starting transfers between devices, shifted(): return lax.ppermute(block, axis, route)  149 us
    unnamed x22, local copies, waits for them, and re-layouts  32.2 us
  transfers between devices with their start and end apart: 33, of which 33 were waited for; matrix products, arithmetic and copies ran while one was open for 3% of the time, Pallas kernels for 0%

commit v1 on v0

v1 whole, which is shorter than its diff:
```python
import functools
import math

import jax
import jax.numpy as jnp
from jax import lax
from jax.experimental import pallas as pl
from jax.experimental.pallas import tpu as pltpu
from jax.sharding import PartitionSpec as P

DH = 128
LOG2E = math.log2(math.e)
ROPE_BASE = 500000.0
MESH = pl.DeviceIdType.MESH
NDP, NCTX = 8, 16
CHIPS = NCTX // 2
f32, bf16 = jnp.float32, jnp.bfloat16


def rope_tables(positions, head_dim):
    half_dim = head_dim // 2
    frequency = ROPE_BASE ** (-2.0 * jnp.arange(half_dim, dtype=f32) / head_dim)
    angles = positions.astype(f32)[:, None] * frequency[None, :]
    return (jnp.cos(angles)[:, None, :], jnp.sin(angles)[:, None, :])


def rotary(values, tables, sign):
    half_dim = values.shape[-1] // 2
    cosine, sine = tables
    a = values[..., :half_dim]
    b = values[..., half_dim:]
    return jnp.concatenate([a * cosine - sign * b * sine, b * cosine + sign * a * sine], axis=-1)


def position():
    dp, ctx = lax.axis_index("dp"), lax.axis_index("ctx")
    return dp // 2, dp % 2, ctx // 4, (ctx // 2) % 2, ctx % 2


def device_at(y, zh, x, zl, core):
    return (y * 2 + zh, x * 4 + zl * 2 + core)


def meet(peers):
    barrier = pltpu.get_barrier_semaphore()
    for peer in peers:
        pl.semaphore_signal(barrier, inc=1, device_id=peer, device_id_type=MESH)
    pl.semaphore_wait(barrier, len(peers))


PARTS = ((0, 384, "zyx"), (384, 384, "yxz"), (768, 256, "xzy"))


def gather_weight_kernel(w_ref, out_ref, own_sem, send, recv, core_send, core_recv):
    y, zh, x, zl, core = position()
    z = zh * 2 + zl

    def peer(axis, step):
        if axis == "x":
            return device_at(y, zh, lax.rem(x + step, 4), zl, core)
        if axis == "y":
            return device_at(lax.rem(y + step, 4), zh, x, zl, core)
        far = lax.rem(z + step, 4)
        return device_at(y, far // 2, x, lax.rem(far, 2), core)

    partner = device_at(y, zh, x, zl, 1 - core)
    meet([peer(axis, step) for axis in "xyz" for step in (1, 2, 3)] + [partner])

    def region(done, start, width):
        yy = slice(None) if "y" in done else y
        xx = slice(None) if "x" in done else x
        zz = slice(None) if "z" in done else z
        return out_ref.at[yy, zz, xx, core, :, pl.ds(start, width)]

    own = pltpu.make_async_copy(w_ref, out_ref.at[y, z, x, core], own_sem)
    own.start()
    own.wait()
    waits = []

    def push(part, phase):
        start, width, order = PARTS[part]
        src = region(order[:phase], start, width)
        copies = []
        for step in (1, 2, 3):
            k = (part * 3 + phase) * 3 + step - 1
            cp = pltpu.make_async_remote_copy(
                src_ref=src, dst_ref=src, send_sem=send.at[k], recv_sem=recv.at[k],
                device_id=peer(order[phase], step), device_id_type=MESH)
            cp.start()
            copies.append(cp)
        return copies

    for phase in range(3):
        current = [push(part, phase) for part in range(3)]
        for copies in current:
            for cp in copies:
                cp.wait_recv()
            waits += copies
    cores = []
    for part in range(3):
        start, width, _ = PARTS[part]
        src = region("xyz", start, width)
        cp = pltpu.make_async_remote_copy(
            src_ref=src, dst_ref=src, send_sem=core_send.at[part], recv_sem=core_recv.at[part],
            device_id=partner, device_id_type=MESH)
        cp.start()
        cores.append(cp)
    for cp in waits:
        cp.wait_send()
    for cp in cores:
        cp.wait()


def gather_weight(w):
    rows, cols = w.shape
    out = pl.pallas_call(
        gather_weight_kernel,
        in_specs=[pl.BlockSpec(memory_space=pl.ANY)],
        out_specs=pl.BlockSpec(memory_space=pl.ANY),
        out_shape=jax.ShapeDtypeStruct((4, 4, 4, 2, rows, cols), w.dtype),
        scratch_shapes=[pltpu.SemaphoreType.DMA, pltpu.SemaphoreType.DMA((27,)), pltpu.SemaphoreType.DMA((27,)),
                        pltpu.SemaphoreType.DMA((3,)), pltpu.SemaphoreType.DMA((3,))],
        compiler_params=pltpu.CompilerParams(collective_id=0, has_side_effects=True),
        name="gather_weight",
    )(w)
    out = out.reshape(4, 2, 2, 4, 2, rows, cols).transpose(0, 1, 3, 2, 4, 5, 6)
    return out.reshape(128 * rows, cols)


def ctx_gather(x_ref, out_ref, own_sem, send, recv, core_send, core_recv):
    dp, ctx = lax.axis_index("dp"), lax.axis_index("ctx")
    chip, core = ctx // 2, ctx % 2
    partner = (dp, chip * 2 + 1 - core)
    own = pltpu.make_async_copy(x_ref, out_ref.at[0], own_sem)
    own.start()
    pushes = []
    for i in range(1, CHIPS):
        cp = pltpu.make_async_remote_copy(
            src_ref=x_ref, dst_ref=out_ref.at[2 * i], send_sem=send.at[i], recv_sem=recv.at[i],
            device_id=(dp, lax.rem(chip + i, CHIPS) * 2 + core), device_id_type=MESH)
        cp.start()
        pushes.append(cp)
    over = []

    def to_partner(i, src):
        slot = lax.rem(2 * i + 1 - 2 * core + NCTX, NCTX)
        cp = pltpu.make_async_remote_copy(
            src_ref=src, dst_ref=out_ref.at[slot], send_sem=core_send.at[i], recv_sem=core_recv.at[i],
            device_id=partner, device_id_type=MESH)
        cp.start()
        over.append(cp)

    to_partner(0, x_ref)
    for i in range(1, CHIPS):
        pushes[i - 1].wait_recv()
        to_partner(i, out_ref.at[2 * i])
    own.wait()
    return pushes, over


def ctx_peers():
    dp, ctx = lax.axis_index("dp"), lax.axis_index("ctx")
    chip, core = ctx // 2, ctx % 2
    return [(dp, lax.rem(chip + i, CHIPS) * 2 + core) for i in range(1, CHIPS)] + [(dp, chip * 2 + 1 - core)]


def gather_ctx_kernel(x_ref, out_ref, own_sem, send, recv, core_send, core_recv):
    meet(ctx_peers())
    pushes, over = ctx_gather(x_ref, out_ref, own_sem, send, recv, core_send, core_recv)
    for cp in pushes:
        cp.wait_send()
    for cp in over:
        cp.wait()


SEMS = [pltpu.SemaphoreType.DMA] + [pltpu.SemaphoreType.DMA((CHIPS,))] * 4


def gather_ctx(x):
    return pl.pallas_call(
        gather_ctx_kernel,
        in_specs=[pl.BlockSpec(memory_space=pl.ANY)],
        out_specs=pl.BlockSpec(memory_space=pl.ANY),
        out_shape=jax.ShapeDtypeStruct((NCTX,) + x.shape, x.dtype),
        scratch_shapes=SEMS,
        compiler_params=pltpu.CompilerParams(collective_id=1, has_side_effects=True),
        name="gather_key_values",
    )(x)


def gather_grad_kernel(x_ref, a_ref, out_ref, b_ref, own_sem, send, recv, core_send, core_recv, own2, a_send, a_recv):
    dp, ctx = lax.axis_index("dp"), lax.axis_index("ctx")
    peers = [(dp, lax.rem(ctx + j, NCTX)) for j in range(1, NCTX)]
    meet(peers)
    keep = pltpu.make_async_copy(a_ref.at[ctx], b_ref.at[0], own2)
    keep.start()
    pushes, over = ctx_gather(x_ref, out_ref, own_sem, send, recv, core_send, core_recv)
    pieces = []
    for j in range(1, NCTX):
        cp = pltpu.make_async_remote_copy(
            src_ref=a_ref.at[lax.rem(ctx + j, NCTX)], dst_ref=b_ref.at[j], send_sem=a_send.at[j], recv_sem=a_recv.at[j],
            device_id=peers[j - 1], device_id_type=MESH)
        cp.start()
        pieces.append(cp)
    for cp in pushes:
        cp.wait_send()
    for cp in over + pieces:
        cp.wait()
    keep.wait()


def gather_grad(x, a):
    return pl.pallas_call(
        gather_grad_kernel,
        in_specs=[pl.BlockSpec(memory_space=pl.ANY)] * 2,
        out_specs=[pl.BlockSpec(memory_space=pl.ANY)] * 2,
        out_shape=[jax.ShapeDtypeStruct((NCTX,) + x.shape, x.dtype), jax.ShapeDtypeStruct(a.shape, a.dtype)],
        scratch_shapes=SEMS + [pltpu.SemaphoreType.DMA] + [pltpu.SemaphoreType.DMA((NCTX,))] * 2,
        compiler_params=pltpu.CompilerParams(collective_id=2, has_side_effects=True),
        name="gather_grad_projected",
    )(x, a)


def reduce_ctx_kernel(g_ref, out_ref, mine, theirs, landed, mine_sem, core_send, core_recv, send, recv):
    dp, ctx = lax.axis_index("dp"), lax.axis_index("ctx")
    chip, core = ctx // 2, ctx % 2
    partner = (dp, chip * 2 + 1 - core)
    meet(ctx_peers())
    order = list(range(1, CHIPS)) + [0]
    loads, swaps = {}, {}
    for i in order:
        other = lax.rem(2 * i + 2 * core - 1 + NCTX, NCTX)
        swaps[i] = pltpu.make_async_remote_copy(
            src_ref=g_ref.at[other], dst_ref=theirs.at[i], send_sem=core_send.at[i], recv_sem=core_recv.at[i],
            device_id=partner, device_id_type=MESH)
        swaps[i].start()
        loads[i] = pltpu.make_async_copy(g_ref.at[2 * i], mine.at[i], mine_sem.at[i])
        loads[i].start()
    pushes = {}
    for i in order:
        loads[i].wait()
        swaps[i].wait_recv()
        total = mine[i].astype(f32) + theirs[i].astype(f32)
        if i == 0:
            out_ref[...] = total
            continue
        mine[i] = total.astype(bf16)
        pushes[i] = pltpu.make_async_remote_copy(
            src_ref=mine.at[i], dst_ref=landed.at[i], send_sem=send.at[i], recv_sem=recv.at[i],
            device_id=(dp, lax.rem(chip + CHIPS - i, CHIPS) * 2 + core), device_id_type=MESH)
        pushes[i].start()
    for i in range(1, CHIPS):
        pushes[i].wait_recv()
        out_ref[...] += landed[i].astype(f32)
    for i in range(1, CHIPS):
        pushes[i].wait_send()
    for i in order:
        swaps[i].wait_send()


def reduce_ctx(g):
    block = g.shape[1:]
    return pl.pallas_call(
        reduce_ctx_kernel,
        in_specs=[pl.BlockSpec(memory_space=pl.ANY)],
        out_specs=pl.BlockSpec(memory_space=pltpu.VMEM),
        out_shape=jax.ShapeDtypeStruct(block, f32),
        scratch_shapes=[pltpu.VMEM((CHIPS,) + block, bf16)] * 3 + [pltpu.SemaphoreType.DMA((CHIPS,))] * 5,
        compiler_params=pltpu.CompilerParams(
            collective_id=3, has_side_effects=True, vmem_limit_bytes=32 * 2**20),
        name="reduce_key_value_grads",
    )(g)


def reduce_dp_kernel(g_ref, out_ref, landed, send, recv):
    dp, ctx = lax.axis_index("dp"), lax.axis_index("ctx")
    peers = [(lax.rem(dp + j, NDP), ctx) for j in range(1, NDP)]
    meet(peers)
    pushes = []
    for j in range(1, NDP):
        cp = pltpu.make_async_remote_copy(
            src_ref=g_ref.at[lax.rem(dp + j, NDP)], dst_ref=landed.at[j], send_sem=send.at[j], recv_sem=recv.at[j],
            device_id=peers[j - 1], device_id_type=MESH)
        cp.start()
        pushes.append(cp)
    total = g_ref[dp]
    for j in range(1, NDP):
        pushes[j - 1].wait_recv()
        total = total + landed[j]
    out_ref[...] = total
    for cp in pushes:
        cp.wait_send()


def reduce_dp(g):
    block = g.shape[1:]
    return pl.pallas_call(
        reduce_dp_kernel,
        in_specs=[pl.BlockSpec(memory_space=pltpu.VMEM)],
        out_specs=pl.BlockSpec(memory_space=pltpu.VMEM),
        out_shape=jax.ShapeDtypeStruct(block, f32),
        scratch_shapes=[pltpu.VMEM((NDP,) + block, f32)] + [pltpu.SemaphoreType.DMA((NDP,))] * 2,
        compiler_params=pltpu.CompilerParams(
            collective_id=4, has_side_effects=True, vmem_limit_bytes=16 * 2**20),
        name="reduce_grad_weight",
    )(g)


def attention_kernel(blocks, heads, chunk, q_ref, do_ref, kv_ref, out_ref, dq_ref, dkv_ref,
                     s_scr, w_scr, kt_scr, vt_scr, dk_acc, dv_acc):
    T = 128
    R = heads * T
    keys = blocks * T
    t = pl.program_id(1)
    c = lax.axis_index("ctx")
    n_chunks = (c * T) // chunk + 1
    scale = DH ** -0.5

    @pl.when(t == 0)
    def _():
        dk_acc[...] = jnp.zeros_like(dk_acc)
        dv_acc[...] = jnp.zeros_like(dv_acc)
        kt_scr[...] = kv_ref[:, :DH].T
        vt_scr[...] = kv_ref[:, DH:].T

    qs = jnp.concatenate([q_ref[:, g*DH:(g+1)*DH] for g in range(heads)], axis=0)
    per = chunk // T

    def scores(i, mask_diag):
        base = pl.multiple_of(i * chunk, chunk)
        k = kv_ref[pl.ds(base, chunk), :DH]
        s = lax.dot_general(k, qs, (((1,), (1,)), ((), ())), preferred_element_type=f32)
        top = None
        for j in range(per):
            part = s[j*T:(j+1)*T]
            if mask_diag and j == 0:
                kk = lax.broadcasted_iota(jnp.int32, (T, R), 0)
                tok = lax.broadcasted_iota(jnp.int32, (T, R), 1) % T
                part = jnp.where(kk <= tok, part, -jnp.inf)
            else:
                part = jnp.where(i * per + j <= c, part, -jnp.inf)
            s_scr[pl.ds(pl.multiple_of(base + j*T, T), T), :] = part
            m = jnp.max(part.reshape(T//8, 8, R), axis=0)
            top = m if top is None else jnp.maximum(top, m)
        return top

    top8 = scores(0, True)
    top8 = lax.fori_loop(1, n_chunks, lambda i, m: jnp.maximum(m, scores(i, False)), top8)
    top = jnp.max(top8, axis=0, keepdims=True)

    def weigh(i, carry):
        acc, tot = carry
        base = pl.multiple_of(i * chunk, chunk)
        s = s_scr[pl.ds(base, chunk), :]
        w = jnp.exp2((s - top) * (scale * LOG2E))
        tot = tot + jnp.sum(w.reshape(chunk//8, 8, R), axis=0)
        wb = w.astype(bf16)
        w_scr[pl.ds(base, chunk), :] = wb
        acc = acc + jnp.dot(vt_scr[:, pl.ds(base, chunk)], wb, preferred_element_type=f32)
        return acc, tot

    acc, tot8 = lax.fori_loop(0, n_chunks, weigh, (jnp.zeros((DH, R), f32), jnp.zeros((8, R), f32)))
    total = jnp.sum(tot8, axis=0, keepdims=True)
    inv = 1.0 / total
    out_t = acc * inv
    out_tb = out_t.astype(bf16).astype(f32)
    do_t = jnp.concatenate([do_ref[:, g*DH:(g+1)*DH].astype(f32).T for g in range(heads)], axis=1)
    dos_t = (do_t * inv).astype(bf16).astype(f32)
    delta = jnp.sum(dos_t * out_tb, axis=0, keepdims=True)
    dos = jnp.concatenate([dos_t[:, g*DH:(g+1)*DH].T for g in range(heads)], axis=0).astype(bf16)
    for g in range(heads):
        out_ref[:, g*DH:(g+1)*DH] = out_tb[:, g*DH:(g+1)*DH].T.astype(bf16)

    def back(i, dq):
        base = pl.multiple_of(i * chunk, chunk)
        v = kv_ref[pl.ds(base, chunk), DH:]
        dp = lax.dot_general(v, dos, (((1,), (1,)), ((), ())), preferred_element_type=f32)
        wb = w_scr[pl.ds(base, chunk), :]
        ds = (dp - delta).astype(bf16) * wb
        dq = dq + jnp.dot(kt_scr[:, pl.ds(base, chunk)], ds, preferred_element_type=f32)
        dk_acc[pl.ds(base, chunk), :] += jnp.dot(ds, qs, preferred_element_type=f32)
        dv_acc[pl.ds(base, chunk), :] += jnp.dot(wb, dos, preferred_element_type=f32)
        return dq

    dq = lax.fori_loop(0, n_chunks, back, jnp.zeros((DH, R), f32)) * scale
    for g in range(heads):
        dq_ref[:, g*DH:(g+1)*DH] = dq[:, g*DH:(g+1)*DH].T.astype(bf16)

    @pl.when(t == pl.num_programs(1) - 1)
    def _():
        dkv_ref[:, :DH] = (dk_acc[...] * scale).astype(bf16)
        dkv_ref[:, DH:] = dv_acc[...].astype(bf16)


def attention(q, do, kv, heads=4, chunk=1024):
    T, HD = q.shape
    keys, width = kv.shape
    kvh = width // (2*DH)
    R = heads*T
    tiles = HD // DH // kvh // heads
    return pl.pallas_call(
        functools.partial(attention_kernel, keys//T, heads, chunk),
        grid=(kvh, tiles),
        in_specs=[pl.BlockSpec((T, heads*DH), lambda h, t: (0, h*tiles+t)),
                  pl.BlockSpec((T, heads*DH), lambda h, t: (0, h*tiles+t)),
                  pl.BlockSpec((keys, 2*DH), lambda h, t: (0, h))],
        out_specs=[pl.BlockSpec((T, heads*DH), lambda h, t: (0, h*tiles+t)),
                   pl.BlockSpec((T, heads*DH), lambda h, t: (0, h*tiles+t)),
                   pl.BlockSpec((keys, 2*DH), lambda h, t: (0, h))],
        out_shape=[jax.ShapeDtypeStruct(q.shape, jnp.bfloat16)]*2 + [jax.ShapeDtypeStruct(kv.shape, jnp.bfloat16)],
        scratch_shapes=[pltpu.VMEM((keys, R), jnp.float32), pltpu.VMEM((keys, R), jnp.bfloat16),
                        pltpu.VMEM((DH, keys), jnp.bfloat16), pltpu.VMEM((DH, keys), jnp.bfloat16),
                        pltpu.VMEM((keys, DH), jnp.float32), pltpu.VMEM((keys, DH), jnp.float32)],
        compiler_params=pltpu.CompilerParams(vmem_limit_bytes=48*2**20),
        name="attention",
    )(q, do, kv)


def on_device(inputs, queries, grad_output, kv_weight):
    tokens = inputs[0]
    count, features = tokens.shape
    width = kv_weight.shape[1]
    half = width // 2
    heads = half // DH
    ctx = lax.axis_index("ctx")
    tables = rope_tables(ctx * count + jnp.arange(count, dtype=jnp.int32), DH)

    weight = gather_weight(kv_weight)
    projected = jnp.dot(tokens, weight, preferred_element_type=f32)
    keys = rotary(projected[:, :half].reshape(count, heads, DH), tables, 1.0).astype(bf16)
    values = projected[:, half:].reshape(count, heads, DH).astype(bf16)
    own = jnp.concatenate([keys, values], axis=-1).reshape(count, width)
    kv = gather_ctx(own).reshape(NCTX * count, width)

    attn_out, grad_query, terms = attention(queries[0], grad_output[0], kv)

    grads = reduce_ctx(terms.reshape(NCTX, count, width)).reshape(count, heads, 2 * DH)
    grad_keys = rotary(grads[..., :DH], tables, -1.0).reshape(count, half)
    grad_values = grads[..., DH:].reshape(count, half)
    grad_projected = jnp.concatenate([grad_keys, grad_values], axis=1).astype(bf16)

    pieces = tokens.reshape(count, NDP, NCTX, -1).transpose(2, 0, 1, 3).reshape(NCTX, count, features // NCTX)
    all_grads, all_tokens = gather_grad(grad_projected, pieces)
    grad_inputs = lax.dot_general(
        grad_projected, weight, (((1,), (1,)), ((), ())), preferred_element_type=f32
    ).astype(bf16)
    part = lax.dot_general(
        all_tokens.reshape(NCTX * count, -1), all_grads.reshape(NCTX * count, width),
        (((0,), (0,)), ((), ())), preferred_element_type=f32)
    grad_weight = reduce_dp(part.reshape(NDP, -1, width))
    return (attn_out[None], grad_query[None], grad_inputs[None], grad_weight)


def solution(mesh):
    tokens = P("dp", "ctx", None)
    rows = P(("dp", "ctx"), None)
    return jax.shard_map(
        on_device, mesh=mesh, in_specs=(tokens, tokens, tokens, rows),
        out_specs=(tokens, tokens, tokens, rows), check_vma=False)
```

time: 1570 us -> 321 us (0.20)
  waiting for transfers between devices: 1170 us -> 0 us
  Pallas kernels: 0 us -> 277 us
  starting transfers between devices: 166 us -> 0 us
  other arithmetic: 90.5 us -> 4.46 us
  local copies, waits for them, and re-layouts: 91.6 us -> 21.2 us
  matrix products: 31.1 us -> 15.3 us
    unnamed x3 -> x0, waiting for transfers between devices: 636 us -> none
    ppermute x31 -> x0, waiting for transfers between devices: 356 us -> none  [the longest x16 336 us: shifted_2(): return lax.ppermute(value, axis, pairs)]
    pallas_call x0 -> x6, Pallas kernels: none -> 277 us  [the longest x1 80.8 us: reduce_ctx(): pl.pallas_call(reduce_ctx_kernel, in_specs=[pl.BlockSpec(memory_space=pl....]
    all_gather x1 -> x0, waiting for transfers between devices: 182 us -> none  [on_device(): weight_all = lax.all_gather(kv_weight, ('dp', 'ctx'), axis=0, tiled=True)]
    ppermute x31 -> x0, starting transfers between devices: 166 us -> none  [the longest x15 149 us: shifted(): return lax.ppermute(block, axis, route)]
    convert_element_type x35 -> x1, other arithmetic: 49.2 us -> 0.01 us  [rope_tables(): angles = positions.astype(f32)[:, None] * frequency[None, :]]
    while x16 -> x0, other arithmetic: 28.9 us -> none
    unnamed x22 -> x18, local copies, waits for them, and re-layouts: 32.2 us -> 6.65 us
  transfers between devices with their start and end apart: 33 -> 0, of which waited for: 33 -> 0; matrix products, arithmetic and copies ran while one was open for 3% -> 0% of each run, Pallas kernels for 0% -> 0%
where the time goes in v1:
time: 321 us; the launch traced here: 319 us
  Pallas kernels  277 us (86%)
  local copies, waits for them, and re-layouts  21.2 us (7%)
  matrix products  15.3 us (5%)
  other arithmetic  4.46 us (1%)
    pallas_call x1, Pallas kernels, reduce_ctx(): pl.pallas_call(reduce_ctx_kernel, in_specs=[pl.BlockSpec(memory_space=pl....  80.8 us
    pallas_call x1, Pallas kernels, gather_grad(): pl.pallas_call(gather_grad_kernel, in_specs=[pl.BlockSpec(memory_space=pl...  53.2 us
    pallas_call x1, Pallas kernels, attention(): pl.pallas_call(functools.partial(attention_kernel, keys // T, heads, chun...  46.2 us
    pallas_call x1, Pallas kernels, gather_weight(): pl.pallas_call(gather_weight_kernel, in_specs=[pl.BlockSpec(memory_space=...  45.4 us
    pallas_call x1, Pallas kernels, gather_ctx(): pl.pallas_call(gather_ctx_kernel, in_specs=[pl.BlockSpec(memory_space=pl....  33.4 us
    pallas_call x1, Pallas kernels, reduce_dp(): pl.pallas_call(reduce_dp_kernel, in_specs=[pl.BlockSpec(memory_space=pltp...  18.3 us
    reshape x1, local copies, waits for them, and re-layouts, gather_weight(): out = out.reshape(4, 2, 2, 4, 2, rows, cols).transpose(0, 1, 3, 2, 4, 5, 6)  8.55 us
    dot_general x1, matrix products, on_device(): lax.dot_general(grad_projected, weight, (((1,), (1,)), ((), ())), preferr...  7.25 us

profile of v1, /device:TPU:0, one launch (start us, length us, event | category | flops | bytes accessed | tf_op | source)
XLA Modules:
  0.0 319.2 jit_solution(13762918147263834022)
XLA Ops:
  0.7 0.9 broadcast_multiply_fusion
  1.6 45.4 %gather_weight.1 = bf16[4,4,4,2,32,1024]{5,4,3,2,1,0:T(8,128)(2,1)} custom-call(bf16[32,1024]{1,0:T(8,128)(2,1)} %w_ref.1), custom_call_target="tpu_custom_call" | custom-call | tf_op jit(solution)/shard_map/gather_weight/pallas_call | solution.py:116
  47.0 0.0 copy-start.3
  47.0 8.6 %copy.10 = bf16[4,2,2,4,2,32,1024]{6,5,4,2,3,1,0:T(8,128)(2,1)} copy(bf16[4,2,2,4,2,32,1024]{6,5,4,3,2,1,0:T(8,128)(2,1)} %bitcast.44) | data formatting | bytes 16777216 | tf_op jit(solution)/shard_map/reshape | solution.py:126
  55.6 0.0 copy-done.3
  55.6 4.6 %fusion.1 = f32[128,1024]{1,0:T(8,128)S(1)} fusion(bf16[4096,1024]{1,0:T(8,128)(2,1)} %bitcast.42, bf16[1,128,4096]{2,1,0:T(8,128)(2,1)S(1)} %copy-done.3), kind=kOutput, calls=%fused_computation.2 | convolution fusion | flops 1073741824 | bytes 9961472 | tf_op jit(solution)/shard_map/dot_general | solution.py:429
  60.2 0.0 copy-start.6
  60.3 0.8 copy-done.6
  61.0 0.0 copy-start.1
  61.0 0.7 slice.33
  61.8 1.1 reshape.109
  62.8 1.8 subtract_convert_fusion.1
  64.6 1.0 slice.51
  65.6 1.3 pad_maximum_fusion
  66.9 0.7 copy.15
  67.6 33.4 %gather_key_values.1 = bf16[16,128,1024]{2,1,0:T(8,128)(2,1)} custom-call(bf16[128,1024]{1,0:T(8,128)(2,1)} %bitcast.48), custom_call_target="tpu_custom_call" | custom-call | tf_op jit(solution)/shard_map/gather_key_values/pallas_call | solution.py:180
  101.0 0.0 copy-done.1
  101.0 0.0 copy-start.2
  101.0 1.6 copy-done.2
  102.6 46.2 %attention.1 = (bf16[128,8192]{1,0:T(8,128)(2,1)}, bf16[128,8192]{1,0:T(8,128)(2,1)}, bf16[2048,1024]{1,0:T(8,128)(2,1)}) custom-call(bf16[128,8192]{1,0:T(8,128)(2,1)S(1)} %bitcast.40, bf16[128,8192]{1,0:T(8,128)(2,1)S(1)} %bitcast.41, bf16[2048,1024]{1,0:T(8,128)(2,1)} %bitcast.45), custom_call_target="tpu_custom_call" | custom-call | tf_op jit(solution)/shard_map/attention/pallas_call | solution.py:401
  148.8 0.0 copy-start
  148.8 2.2 copy-done
  151.0 80.8 %reduce_key_value_grads.1 = f32[128,1024]{1,0:T(8,128)S(1)} custom-call(bf16[16,128,1024]{2,1,0:T(8,128)(2,1)S(1)} %bitcast.39), custom_call_target="tpu_custom_call" | custom-call | tf_op jit(solution)/shard_map/reduce_key_value_grads/pallas_call | solution.py:263
  231.8 0.2 reshape.113
  232.1 0.3 subtract_convert_fusion
  232.4 0.2 pad_maximum_fusion.1
  232.7 0.0 copy-start.4
  232.7 0.7 copy.11
  233.4 0.1 copy.12
  233.5 1.3 copy.13.a_ref
  234.8 0.0 copy-done.4
  234.8 53.2 %gather_grad_projected.1 = (bf16[16,128,1024]{2,1,0:T(8,128)(2,1)}, bf16[16,128,256]{2,1,0:T(8,128)(2,1)}) custom-call(bf16[128,1024]{1,0:T(8,128)(2,1)} %copy-done.4, bf16[16,128,256]{2,1,0:T(8,128)(2,1)} %copy.13.a_ref), custom_call_target="tpu_custom_call" | custom-call | tf_op jit(solution)/shard_map/gather_grad_projected/pallas_call | solution.py:213
  288.0 1.5 copy.14
  289.5 0.0 copy-start.5
  289.5 3.5 %fusion.3.g_ref = f32[8,32,1024]{2,1,0:T(8,128)S(1)} fusion(bf16[8,32,2048]{2,1,0:T(8,128)(2,1)S(1)} %bitcast.50, bf16[2048,1024,1]{1,0,2:T(8,128)(2,1)} %bitcast.54), kind=kOutput, calls=%fused_computation.19 | convolution fusion | flops 1073741824 | bytes 6291456 | tf_op jit(solution)/shard_map/dot_general | solution.py:447
  293.0 18.3 %reduce_grad_weight.1 = f32[32,1024]{1,0:T(8,128)S(1)} custom-call(f32[8,32,1024]{2,1,0:T(8,128)S(1)} %fusion.3.g_ref), custom_call_target="tpu_custom_call" | custom-call | tf_op jit(solution)/shard_map/reduce_grad_weight/pallas_call | solution.py:297
  311.3 0.0 copy-done.5
  311.3 7.2 %fusion = bf16[1,128,4096]{2,1,0:T(8,128)(2,1)} fusion(bf16[128,1024]{1,0:T(8,128)(2,1)S(1)} %copy-done.5, bf16[4096,1024]{1,0:T(8,128)(2,1)} %bitcast.43), kind=kOutput, calls=%fused_computation.1 | convolution fusion | flops 1074266112 | bytes 9699328 | tf_op jit(solution)/shard_map/dot_general | solution.py:444
  318.5 0.7 copy.22
  (6 shorter events, 0.1 us)
Async XLA Ops:
  47.0 8.6 %copy-start.3 = (bf16[1,128,4096]{2,1,0:T(8,128)(2,1)S(1)}, bf16[1,128,4096]{2,1,0:T(8,128)(2,1)}, u32[]{:S(2)}) copy-start(bf16[1,128,4096]{2,1,0:T(8,128)(2,1)} %param.4) | copy-start | bytes 3145732
  60.2 0.8 copy-start.6
  61.0 39.9 %copy-start.1 = (bf16[1,128,8192]{2,1,0:T(8,128)(2,1)S(1)}, bf16[1,128,8192]{2,1,0:T(8,128)(2,1)}, u32[]{:S(2)}) copy-start(bf16[1,128,8192]{2,1,0:T(8,128)(2,1)} %param.5) | copy-start | bytes 6291460
  101.0 1.6 copy-start.2
  148.8 2.2 copy-start
  232.7 2.1 copy-start.4
  289.5 21.8 %copy-start.5 = (bf16[128,1024]{1,0:T(8,128)(2,1)S(1)}, bf16[128,1024]{1,0:T(8,128)(2,1)}, u32[]{:S(2)}) copy-start(bf16[128,1024]{1,0:T(8,128)(2,1)} %copy-done.4) | copy-start | bytes 786436

commit v2 on v1

v2 whole, which is shorter than its diff:
```python
import functools
import math

import jax
import jax.numpy as jnp
from jax import lax
from jax.experimental import pallas as pl
from jax.experimental.pallas import tpu as pltpu
from jax.sharding import PartitionSpec as P

DH = 128
LOG2E = math.log2(math.e)
ROPE_BASE = 500000.0
MESH = pl.DeviceIdType.MESH
NDP, NCTX = 8, 16
CHIPS = NCTX // 2
f32, bf16 = jnp.float32, jnp.bfloat16


def rope_tables(positions, head_dim):
    half_dim = head_dim // 2
    frequency = ROPE_BASE ** (-2.0 * jnp.arange(half_dim, dtype=f32) / head_dim)
    angles = positions.astype(f32)[:, None] * frequency[None, :]
    return (jnp.cos(angles)[:, None, :], jnp.sin(angles)[:, None, :])


def rotary(values, tables, sign):
    half_dim = values.shape[-1] // 2
    cosine, sine = tables
    a = values[..., :half_dim]
    b = values[..., half_dim:]
    return jnp.concatenate([a * cosine - sign * b * sine, b * cosine + sign * a * sine], axis=-1)


def position():
    dp, ctx = lax.axis_index("dp"), lax.axis_index("ctx")
    return dp // 2, dp % 2, ctx // 4, (ctx // 2) % 2, ctx % 2


def device_at(y, zh, x, zl, core):
    return (y * 2 + zh, x * 4 + zl * 2 + core)


def meet(peers):
    barrier = pltpu.get_barrier_semaphore()
    for peer in peers:
        pl.semaphore_signal(barrier, inc=1, device_id=peer, device_id_type=MESH)
    pl.semaphore_wait(barrier, len(peers))


PARTS = ((0, 384, "zyx"), (384, 384, "yxz"), (768, 256, "xzy"))


def gather_weight_kernel(w_ref, out_ref, own_sem, send, recv, core_send, core_recv):
    y, zh, x, zl, core = position()
    z = zh * 2 + zl

    def peer(axis, step):
        if axis == "x":
            return device_at(y, zh, lax.rem(x + step, 4), zl, core)
        if axis == "y":
            return device_at(lax.rem(y + step, 4), zh, x, zl, core)
        far = lax.rem(z + step, 4)
        return device_at(y, far // 2, x, lax.rem(far, 2), core)

    partner = device_at(y, zh, x, zl, 1 - core)
    meet([peer(axis, step) for axis in "xyz" for step in (1, 2, 3)] + [partner])

    def region(done, start, width):
        yy = slice(None) if "y" in done else y
        xx = slice(None) if "x" in done else x
        zh_, zl_ = (slice(None), slice(None)) if "z" in done else (zh, zl)
        return out_ref.at[yy, zh_, xx, zl_, core, :, pl.ds(start, width)]

    own = pltpu.make_async_copy(w_ref, out_ref.at[y, zh, x, zl, core], own_sem)
    own.start()
    own.wait()
    waits = []

    def push(part, phase):
        start, width, order = PARTS[part]
        src = region(order[:phase], start, width)
        copies = []
        for step in (1, 2, 3):
            k = (part * 3 + phase) * 3 + step - 1
            cp = pltpu.make_async_remote_copy(
                src_ref=src, dst_ref=src, send_sem=send.at[k], recv_sem=recv.at[k],
                device_id=peer(order[phase], step), device_id_type=MESH)
            cp.start()
            copies.append(cp)
        return copies

    for phase in range(3):
        current = [push(part, phase) for part in range(3)]
        for copies in current:
            for cp in copies:
                cp.wait_recv()
            waits += copies
    cores = []
    for part in range(3):
        start, width, _ = PARTS[part]
        src = region("xyz", start, width)
        cp = pltpu.make_async_remote_copy(
            src_ref=src, dst_ref=src, send_sem=core_send.at[part], recv_sem=core_recv.at[part],
            device_id=partner, device_id_type=MESH)
        cp.start()
        cores.append(cp)
    for cp in waits:
        cp.wait_send()
    for cp in cores:
        cp.wait()


def gather_weight(w):
    rows, cols = w.shape
    out = pl.pallas_call(
        gather_weight_kernel,
        in_specs=[pl.BlockSpec(memory_space=pl.ANY)],
        out_specs=pl.BlockSpec(memory_space=pl.ANY),
        out_shape=jax.ShapeDtypeStruct((4, 2, 4, 2, 2, rows, cols), w.dtype),
        scratch_shapes=[pltpu.SemaphoreType.DMA, pltpu.SemaphoreType.DMA((27,)), pltpu.SemaphoreType.DMA((27,)),
                        pltpu.SemaphoreType.DMA((3,)), pltpu.SemaphoreType.DMA((3,))],
        compiler_params=pltpu.CompilerParams(collective_id=0, has_side_effects=True),
        name="gather_weight",
    )(w)
    return out.reshape(128 * rows, cols)


QHEADS = 4
KVH = 4
T = 128


def main_kernel(tiles, q_ref, do_ref, own_ref, tok_ref, w_hbm, cos_ref, sin_ref,
                out_ref, dq_ref, gin_ref, gw_ref,
                kv, s_scr, wt_scr, kt_scr, vt_scr, dk_acc, dv_acc,
                even, odd, theirs, landed, own32, gp_all, gp_own, weight, tok_all, tok_t, dw, dw_landed,
                local, kv_send, kv_recv, fw_send, fw_recv, swap_send, swap_recv, ps_send, ps_recv,
                ag_send, ag_recv, agf_send, agf_recv, dw_send, dw_recv, a_send, a_recv):
    dp, c = lax.axis_index("dp"), lax.axis_index("ctx")
    chip, core = c // 2, c % 2
    partner = (dp, chip * 2 + 1 - core)
    h, t = pl.program_id(0), pl.program_id(1)
    R = QHEADS * T
    keys = NCTX * T
    scale = DH ** -0.5
    far = list(range(1, CHIPS))

    def chip_at(i):
        return (dp, lax.rem(chip + i + CHIPS, CHIPS) * 2 + core)

    def remote(src, dst, send, recv, device):
        return pltpu.make_async_remote_copy(
            src_ref=src, dst_ref=dst, send_sem=send, recv_sem=recv, device_id=device, device_id_type=MESH)

    def kv_push(hd, i):
        return remote(own_ref.at[hd], kv.at[hd, 2 * i], kv_send.at[hd, i], kv_recv.at[hd, i], chip_at(i))

    def kv_own(hd):
        return remote(own_ref.at[hd], kv.at[hd, 1], fw_send.at[hd, 0], fw_recv.at[hd, 0], partner)

    def kv_forward(hd, i):
        return remote(kv.at[hd, 2 * i], kv.at[hd, 2 * i + 1 - 2 * core], fw_send.at[hd, i], fw_recv.at[hd, i], partner)

    def swap(hd):
        return remote(odd.at[hd], theirs.at[hd], swap_send.at[hd], swap_recv.at[hd], partner)

    def sum_push(hd, i):
        return remote(even.at[hd, i], landed.at[hd, i], ps_send.at[hd, i], ps_recv.at[hd, i], chip_at(-i))

    def gp_push(hd, i):
        return remote(gp_all.at[hd, 0], gp_all.at[hd, 2 * i], ag_send.at[hd, i], ag_recv.at[hd, i], chip_at(i))

    def gp_forward(hd, i):
        slot = lax.rem(2 * i + 1 - 2 * core + NCTX, NCTX)
        return remote(gp_all.at[hd, 2 * i], gp_all.at[hd, slot], agf_send.at[hd, i], agf_recv.at[hd, i], partner)

    def tok_push(j):
        to = lax.rem(c + j, NCTX)
        return remote(tok_ref.at[to], tok_all.at[j], a_send.at[j], a_recv.at[j], (dp, to))

    def dw_push(hd, j):
        to = lax.rem(dp + j, NDP)
        return remote(dw.at[hd, to], dw_landed.at[hd, j], dw_send.at[hd, j], dw_recv.at[hd, j], (to, c))

    own_copy = pltpu.make_async_copy(own_ref, kv.at[:, 0], local.at[0])
    weight_copy = pltpu.make_async_copy(w_hbm, weight, local.at[1])
    tok_copy = pltpu.make_async_copy(tok_ref.at[c], tok_all.at[0], local.at[2])

    def forward_keys(hd):
        for i in far:
            @pl.when(i <= chip)
            def _():
                kv_push(hd, i).wait_recv()
                kv_forward(hd, i).start()

    def await_keys(hd):
        for i in far:
            @pl.when(i <= chip)
            def _():
                kv_forward(hd, i).wait_recv()

        @pl.when(core == 1)
        def _():
            kv_own(hd).wait_recv()

    def add_pair(hd):
        swap(hd).wait_recv()
        own32[...] = even[hd, 0].astype(f32) + theirs[hd, lax.rem(CHIPS - core, CHIPS)].astype(f32)
        for i in far:
            @pl.when(i <= chip)
            def _():
                total = even[hd, i].astype(f32) + theirs[hd, i - core].astype(f32)
                even[hd, i] = total.astype(bf16)
                sum_push(hd, i).start()

    def finish_block(hd):
        for i in far:
            @pl.when(chip + i < CHIPS)
            def _():
                sum_push(hd, i).wait_recv()
                own32[...] += landed[hd, i].astype(f32)
        key_part = own32[:, :DH]
        key_part = (key_part * cos_ref[...] + pltpu.roll(key_part, DH // 2, 1) * sin_ref[...]).astype(bf16)
        value_part = own32[:, DH:].astype(bf16)
        gp_all[hd, 0, :, :DH] = key_part
        gp_all[hd, 0, :, DH:] = value_part
        gp_own[hd] = key_part
        gp_own[KVH + hd] = value_part
        for i in far:
            gp_push(hd, i).start()
        gp_forward(hd, 0).start()

    def forward_grads(hd):
        for i in far:
            gp_push(hd, i).wait_recv()
            gp_forward(hd, i).start()

    def weight_grad(hd):
        for i in range(CHIPS):
            gp_forward(hd, i).wait_recv()
        part = jnp.dot(tok_t[...], gp_all[hd].reshape(keys, 2 * DH), preferred_element_type=f32)
        dw[hd] = part.reshape(dw.shape[1:])
        for j in range(1, NDP):
            dw_push(hd, j).start()

    @pl.when((h == 0) & (t == 0))
    def _():
        meet([(dp, lax.rem(c + j, NCTX)) for j in range(1, NCTX)]
             + [(lax.rem(dp + j, NDP), c) for j in range(1, NDP)])
        own_copy.start()
        for hd in range(KVH):
            for i in far:
                @pl.when(chip + i < CHIPS)
                def _():
                    kv_push(hd, i).start()

            @pl.when(core == 0)
            def _():
                kv_own(hd).start()
        weight_copy.start()
        tok_copy.start()
        for j in range(1, NCTX):
            tok_push(j).start()
        for j in range(1, NCTX):
            @pl.when(j > c)
            def _():
                kv[:, j] = jnp.zeros((KVH, T, 2 * DH), bf16)
        own_copy.wait()
        forward_keys(0)

    @pl.when(t == 0)
    def _():
        await_keys(h)
        dk_acc[...] = jnp.zeros_like(dk_acc)
        dv_acc[...] = jnp.zeros_like(dv_acc)
        kt_scr[...] = kv[h, :, :, :DH].reshape(keys, DH).T
        vt_scr[...] = kv[h, :, :, DH:].reshape(keys, DH).T

    qs = jnp.concatenate([q_ref[:, g*DH:(g+1)*DH] for g in range(QHEADS)], axis=0)
    k = kv[h, :, :, :DH].reshape(keys, DH)
    v = kv[h, :, :, DH:].reshape(keys, DH)
    s = lax.dot_general(k, qs, (((1,), (1,)), ((), ())), preferred_element_type=f32)
    top = None
    for j in range(NCTX):
        part = s[j*T:(j+1)*T]
        if j == 0:
            key = lax.broadcasted_iota(jnp.int32, (T, R), 0)
            token = lax.broadcasted_iota(jnp.int32, (T, R), 1) % T
            part = jnp.where(key <= token, part, -jnp.inf)
        else:
            part = jnp.where(j <= c, part, -jnp.inf)
        s_scr[pl.ds(j*T, T), :] = part
        best = jnp.max(part.reshape(T//8, 8, R), axis=0)
        top = best if top is None else jnp.maximum(top, best)
    top = jnp.max(top, axis=0, keepdims=True)

    weights = jnp.exp2((s_scr[...] - top) * (scale * LOG2E))
    total = jnp.sum(jnp.sum(weights.reshape(keys//8, 8, R), axis=0), axis=0, keepdims=True)
    wt_scr[...] = weights.astype(bf16)
    acc = jnp.dot(vt_scr[...], wt_scr[...], preferred_element_type=f32)
    inv = 1.0 / total
    out_t = (acc * inv).astype(bf16).astype(f32)
    do_t = jnp.concatenate([do_ref[:, g*DH:(g+1)*DH].astype(f32).T for g in range(QHEADS)], axis=1)
    dos_t = (do_t * inv).astype(bf16).astype(f32)
    delta = jnp.sum(dos_t * out_t, axis=0, keepdims=True)
    dos = jnp.concatenate([dos_t[:, g*DH:(g+1)*DH].T for g in range(QHEADS)], axis=0).astype(bf16)
    for g in range(QHEADS):
        out_ref[:, g*DH:(g+1)*DH] = out_t[:, g*DH:(g+1)*DH].T.astype(bf16)

    dprobs = lax.dot_general(v, dos, (((1,), (1,)), ((), ())), preferred_element_type=f32)
    wb = wt_scr[...]
    ds = (dprobs - delta).astype(bf16) * wb
    dq = jnp.dot(kt_scr[...], ds, preferred_element_type=f32) * scale
    dk_acc[...] += jnp.dot(ds, qs, preferred_element_type=f32)
    dv_acc[...] += jnp.dot(wb, dos, preferred_element_type=f32)
    for g in range(QHEADS):
        dq_ref[:, g*DH:(g+1)*DH] = dq[:, g*DH:(g+1)*DH].T.astype(bf16)

    @pl.when((t == 0) & (h >= 1))
    def _():
        add_pair(h - 1)

    @pl.when((t == 0) & (h >= 2))
    def _():
        forward_grads(h - 2)

    @pl.when((t == 1) & (h < KVH - 1))
    def _():
        forward_keys(h + 1)

    @pl.when((t == 1) & (h == 1))
    def _():
        tok_copy.wait()
        for j in range(1, NCTX):
            tok_push(j).wait_recv()
        tok_t[...] = tok_all[...].reshape(keys, -1).T

    @pl.when((t == 2) & (h >= 1))
    def _():
        finish_block(h - 1)

    @pl.when((t == 2) & (h >= 2))
    def _():
        weight_grad(h - 2)

    @pl.when(t == tiles - 1)
    def _():
        for q in range(CHIPS):
            for parity, ref in ((0, even), (1, odd)):
                rows = pl.ds((2 * q + parity) * T, T)
                ref[h, q, :, :DH] = (dk_acc[rows, :] * scale).astype(bf16)
                ref[h, q, :, DH:] = dv_acc[rows, :].astype(bf16)
        swap(h).start()

    @pl.when((t == tiles - 1) & (h == KVH - 1))
    def _():
        last = KVH - 1
        forward_grads(last - 1)
        add_pair(last)
        weight_grad(last - 1)
        finish_block(last)
        weight_copy.wait()
        gp = jnp.concatenate([gp_own[n] for n in range(2 * KVH)], axis=1)
        block = 512

        def inputs_part(n, carry):
            rows = pl.ds(pl.multiple_of(n * block, block), block)
            gin_ref[:, rows] = lax.dot_general(
                gp, weight[rows, :], (((1,), (1,)), ((), ())), preferred_element_type=f32).astype(bf16)
            return carry

        lax.fori_loop(0, weight.shape[0] // block, inputs_part, 0)
        forward_grads(last)
        weight_grad(last)
        for hd in range(KVH):
            total_w = dw[hd, dp]
            for j in range(1, NDP):
                dw_push(hd, j).wait_recv()
                total_w = total_w + dw_landed[hd, j]
            gw_ref[:, hd*DH:(hd+1)*DH] = total_w[:, :DH]
            gw_ref[:, (KVH+hd)*DH:(KVH+hd+1)*DH] = total_w[:, DH:]
        for hd in range(KVH):
            for i in far:
                @pl.when(chip + i < CHIPS)
                def _():
                    kv_push(hd, i).wait_send()

                @pl.when(i <= chip)
                def _():
                    kv_forward(hd, i).wait_send()
                    sum_push(hd, i).wait_send()

                gp_push(hd, i).wait_send()

            @pl.when(core == 0)
            def _():
                kv_own(hd).wait_send()

            swap(hd).wait_send()
            for i in range(CHIPS):
                gp_forward(hd, i).wait_send()
            for j in range(1, NDP):
                dw_push(hd, j).wait_send()
        for j in range(1, NCTX):
            tok_push(j).wait_send()


def main(q, do, own, pieces, weight, cosine, sine):
    tiles = q.shape[1] // DH // KVH // QHEADS
    keys, R = NCTX * T, QHEADS * T
    tile = pl.BlockSpec((T, R), lambda h, t: (0, h * tiles + t))
    hbm = pl.BlockSpec(memory_space=pl.ANY)
    table = pl.BlockSpec((T, DH), lambda h, t: (0, 0))
    features, width = weight.shape
    per = features // NCTX
    rows = per // NDP
    dma = pltpu.SemaphoreType.DMA
    return pl.pallas_call(
        functools.partial(main_kernel, tiles),
        grid=(KVH, tiles),
        in_specs=[tile, tile, hbm, hbm, hbm, table, table],
        out_specs=[tile, tile,
                   pl.BlockSpec((T, features), lambda h, t: (0, 0)),
                   pl.BlockSpec((rows, width), lambda h, t: (0, 0))],
        out_shape=[jax.ShapeDtypeStruct(q.shape, bf16), jax.ShapeDtypeStruct(q.shape, bf16),
                   jax.ShapeDtypeStruct((T, features), bf16), jax.ShapeDtypeStruct((rows, width), f32)],
        scratch_shapes=[
            pltpu.VMEM((KVH, NCTX, T, 2 * DH), bf16),
            pltpu.VMEM((keys, R), f32), pltpu.VMEM((keys, R), bf16),
            pltpu.VMEM((DH, keys), bf16), pltpu.VMEM((DH, keys), bf16),
            pltpu.VMEM((keys, DH), f32), pltpu.VMEM((keys, DH), f32),
            pltpu.VMEM((KVH, CHIPS, T, 2 * DH), bf16),
            pltpu.VMEM((KVH, CHIPS, T, 2 * DH), bf16),
            pltpu.VMEM((KVH, CHIPS, T, 2 * DH), bf16),
            pltpu.VMEM((KVH, CHIPS, T, 2 * DH), bf16),
            pltpu.VMEM((T, 2 * DH), f32),
            pltpu.VMEM((KVH, NCTX, T, 2 * DH), bf16),
            pltpu.VMEM((2 * KVH, T, DH), bf16),
            pltpu.VMEM((features, width), bf16),
            pltpu.VMEM((NCTX, T, per), bf16), pltpu.VMEM((per, keys), bf16),
            pltpu.VMEM((KVH, NDP, rows, 2 * DH), f32), pltpu.VMEM((KVH, NDP, rows, 2 * DH), f32),
            dma((3,)), dma((KVH, CHIPS)), dma((KVH, CHIPS)), dma((KVH, CHIPS)), dma((KVH, CHIPS)),
            dma((KVH,)), dma((KVH,)), dma((KVH, CHIPS)), dma((KVH, CHIPS)),
            dma((KVH, CHIPS)), dma((KVH, CHIPS)), dma((KVH, CHIPS)), dma((KVH, CHIPS)),
            dma((KVH, NDP)), dma((KVH, NDP)), dma((NCTX,)), dma((NCTX,))],
        compiler_params=pltpu.CompilerParams(
            collective_id=1, has_side_effects=True, vmem_limit_bytes=58 * 2**20),
        name="attention_and_exchanges",
    )(q, do, own, pieces, weight, cosine, sine)


def on_device(inputs, queries, grad_output, kv_weight):
    tokens = inputs[0]
    count, features = tokens.shape
    half = kv_weight.shape[1] // 2
    heads = half // DH
    ctx = lax.axis_index("ctx")
    cosine, sine = rope_tables(ctx * count + jnp.arange(count, dtype=jnp.int32), DH)

    weight = gather_weight(kv_weight)
    projected = jnp.dot(tokens, weight, preferred_element_type=f32)
    keys = rotary(projected[:, :half].reshape(count, heads, DH), (cosine, sine), 1.0).astype(bf16)
    values = projected[:, half:].reshape(count, heads, DH).astype(bf16)
    own = jnp.concatenate([keys, values], axis=-1).transpose(1, 0, 2)
    pieces = tokens.reshape(count, NDP, NCTX, -1).transpose(2, 0, 1, 3).reshape(NCTX, count, features // NCTX)
    cosine, sine = cosine[:, 0], sine[:, 0]
    attn_out, grad_query, grad_inputs, grad_weight = main(
        queries[0], grad_output[0], own, pieces, weight,
        jnp.concatenate([cosine, cosine], axis=1), jnp.concatenate([sine, -sine], axis=1))
    return (attn_out[None], grad_query[None], grad_inputs[None], grad_weight)


def solution(mesh):
    tokens = P("dp", "ctx", None)
    rows = P(("dp", "ctx"), None)
    return jax.shard_map(
        on_device, mesh=mesh, in_specs=(tokens, tokens, tokens, rows),
        out_specs=(tokens, tokens, tokens, rows), check_vma=False)
```

time: 321 us -> 201 us (0.63)
  Pallas kernels: 277 us -> 181 us
  matrix products: 15.3 us -> 4.63 us
  local copies, waits for them, and re-layouts: 21.2 us -> 10.6 us
    pallas_call x5 -> x1, Pallas kernels: 232 us -> 136 us  [main(): pl.pallas_call(functools.partial(main_kernel, tiles), grid=(KVH, tiles),...]
    dot_general x2 -> x0, matrix products: 10.7 us -> none  [the longest x1 7.25 us: on_device(): lax.dot_general(grad_projected, weight, (((1,), (1,)), ((), ())), preferr...]
    reshape x3 -> x0, local copies, waits for them, and re-layouts: 9.87 us -> none  [the longest x1 8.55 us: gather_weight(): out = out.reshape(4, 2, 2, 4, 2, rows, cols).transpose(0, 1, 3, 2, 4, 5, 6)]
    unnamed x18 -> x15, local copies, waits for them, and re-layouts: 6.65 us -> 8.7 us
where the time goes in v2:
time: 201 us; the launch traced here: 199 us
  Pallas kernels  181 us (90%)
  local copies, waits for them, and re-layouts  10.6 us (5%)
  matrix products  4.63 us (2%)
    pallas_call x1, Pallas kernels, main(): pl.pallas_call(functools.partial(main_kernel, tiles), grid=(KVH, tiles),...  136 us
    pallas_call x1, Pallas kernels, gather_weight(): pl.pallas_call(gather_weight_kernel, in_specs=[pl.BlockSpec(memory_space=...  45.4 us
    unnamed x15, local copies, waits for them, and re-layouts  8.7 us
    dot_general x1, matrix products, on_device(): projected = jnp.dot(tokens, weight, preferred_element_type=f32)  4.63 us

profile of v2, /device:TPU:0, one launch (start us, length us, event | category | flops | bytes accessed | tf_op | source)
XLA Modules:
  0.0 198.9 jit_solution(1187642681467768287)
XLA Ops:
  0.7 0.3 fusion.2
  1.0 0.8 pad_maximum_fusion
  1.7 1.6 copy.14
  3.4 0.1 copy.15
  3.5 1.3 copy.16.tok_ref
  4.8 0.0 copy-start
  4.8 45.4 %gather_weight.1 = bf16[4,2,4,2,2,32,1024]{6,5,4,3,2,1,0:T(8,128)(2,1)} custom-call(bf16[32,1024]{1,0:T(8,128)(2,1)} %w_ref.1), custom_call_target="tpu_custom_call" | custom-call | tf_op jit(solution)/shard_map/gather_weight/pallas_call | solution.py:116
  50.2 0.0 copy-done
  50.2 4.6 %fusion = f32[128,1024]{1,0:T(8,128)S(1)} fusion(bf16[4096,1024]{1,0:T(8,128)(2,1)} %bitcast.18, bf16[1,128,4096]{2,1,0:T(8,128)(2,1)S(1)} %copy-done), kind=kOutput, calls=%fused_computation | convolution fusion | flops 1073741824 | bytes 9961472 | tf_op jit(solution)/shard_map/dot_general | solution.py:462
  54.9 0.1 copy.9
  55.0 0.1 copy.12
  55.2 0.1 copy.13
  55.3 0.1 copy.18
  55.5 0.1 copy.17
  55.6 0.1 subtract_convert_fusion
  55.7 0.9 maximum_bitcast_fusion.own_ref
  56.6 135.5 %attention_and_exchanges.1 = (bf16[128,8192]{1,0:T(8,128)(2,1)}, bf16[128,8192]{1,0:T(8,128)(2,1)}, bf16[128,4096]{1,0:T(8,128)(2,1)}, f32[32,1024]{1,0:T(8,128)}) custom-call(bf16[128,8192]{1,0:T(8,128)(2,1)} %bitcast.24, bf16[128,8192]{1,0:T(8,128)(2,1)} %bitcast.25, bf16[4,128,256]{2,1,0:T(8,128)(2,1)} %maximum_bitcast_fusion.own_ref, ...), custom_call_target="tpu_custom_call" | custom-call | tf_op jit(solution)/shard_map/attention_and_exchanges/pallas_call | solution.py:419
  192.1 0.0 copy-start.1
  192.1 3.2 %copy.23 = bf16[1,128,8192]{2,1,0:T(8,128)(2,1)} copy(bf16[1,128,8192]{2,1,0:T(8,128)(2,1)} %bitcast.23) | data formatting | bytes 4194304
  195.3 0.0 copy-done.1
  195.3 0.0 copy-start.2
  195.3 0.0 copy-start.3
  195.3 1.3 copy.24
  196.7 0.6 copy-done.2
  197.3 1.0 copy.25
  198.3 0.0 copy-done.3
  198.3 0.7 copy.26
  (5 shorter events, 0.1 us)
Async XLA Ops:
  4.8 45.4 %copy-start = (bf16[1,128,4096]{2,1,0:T(8,128)(2,1)S(1)}, bf16[1,128,4096]{2,1,0:T(8,128)(2,1)}, u32[]{:S(2)}) copy-start(bf16[1,128,4096]{2,1,0:T(8,128)(2,1)} %param.4) | copy-start | bytes 3145732
  192.1 3.3 %copy-start.1 = (bf16[128,8192]{1,0:T(8,128)(2,1)S(1)}, bf16[128,8192]{1,0:T(8,128)(2,1)}, u32[]{:S(2)}) copy-start(bf16[128,8192]{1,0:T(8,128)(2,1)} %get-tuple-element.9) | copy-start | bytes 6291460
  195.3 2.0 copy-start.2
  195.3 2.9 %copy-start.3 = (f32[32,1024]{1,0:T(8,128)S(1)}, f32[32,1024]{1,0:T(8,128)}, u32[]{:S(2)}) copy-start(f32[32,1024]{1,0:T(8,128)} %get-tuple-element.28) | copy-start | bytes 393220

commit v3 on v2

v3 whole, which is shorter than its diff:
```python
import functools
import math

import jax
import jax.numpy as jnp
from jax import lax
from jax.experimental import pallas as pl
from jax.experimental.pallas import tpu as pltpu
from jax.sharding import PartitionSpec as P

DH = 128
LOG2E = math.log2(math.e)
ROPE_BASE = 500000.0
MESH = pl.DeviceIdType.MESH
NDP, NCTX = 8, 16
CHIPS = NCTX // 2
f32, bf16 = jnp.float32, jnp.bfloat16


def rope_tables(positions, head_dim):
    half_dim = head_dim // 2
    frequency = ROPE_BASE ** (-2.0 * jnp.arange(half_dim, dtype=f32) / head_dim)
    angles = positions.astype(f32)[:, None] * frequency[None, :]
    return jnp.cos(angles), jnp.sin(angles)


def position():
    dp, ctx = lax.axis_index("dp"), lax.axis_index("ctx")
    return dp // 2, dp % 2, ctx // 4, (ctx // 2) % 2, ctx % 2


def device_at(y, zh, x, zl, core):
    return (y * 2 + zh, x * 4 + zl * 2 + core)


def meet(peers):
    barrier = pltpu.get_barrier_semaphore()
    for peer in peers:
        pl.semaphore_signal(barrier, inc=1, device_id=peer, device_id_type=MESH)
    pl.semaphore_wait(barrier, len(peers))


QHEADS = 4
KVH = 4
T = 128


def main_kernel(tiles, q_ref, do_ref, tok_ref, w_ref, cos_ref, sin_ref,
                out_ref, dq_ref, gin_ref, gw_ref,
                kv, s_scr, wt_scr, kt_scr, vt_scr, dk_acc, dv_acc,
                even, odd, theirs, landed, own32, gp_all, gp_own, weight, tok_own, tok_t, dw, dw_landed,
                w_send, w_recv, ws_send, ws_recv, tok_local, kv_send, kv_recv, fw_send, fw_recv, swap_send, swap_recv, ps_send, ps_recv,
                ag_send, ag_recv, agf_send, agf_recv, dw_send, dw_recv, a_send, a_recv):
    dp, c = lax.axis_index("dp"), lax.axis_index("ctx")
    chip, core = c // 2, c % 2
    partner = (dp, chip * 2 + 1 - core)
    h, t = pl.program_id(0), pl.program_id(1)
    R = QHEADS * T
    keys = NCTX * T
    scale = DH ** -0.5
    far = list(range(1, CHIPS))
    y, zh, x, zl, _ = position()
    z = zh * 2 + zl

    def chip_at(i):
        return (dp, lax.rem(chip + i + CHIPS, CHIPS) * 2 + core)

    def remote(src, dst, send, recv, device):
        return pltpu.make_async_remote_copy(
            src_ref=src, dst_ref=dst, send_sem=send, recv_sem=recv, device_id=device, device_id_type=MESH)

    def w_axes(hd, u):
        return ("zyx", "yxz", "xzy")[(2 * hd + u) % 3]

    def along(axis, step):
        if axis == "x":
            return device_at(y, zh, lax.rem(x + step, 4), zl, core)
        if axis == "y":
            return device_at(lax.rem(y + step, 4), zh, x, zl, core)
        to = lax.rem(z + step, 4)
        return device_at(y, to // 2, x, lax.rem(to, 2), core)

    def w_region(hd, u, done):
        yy = slice(None) if "y" in done else y
        xx = slice(None) if "x" in done else x
        zz, zzl = (slice(None), slice(None)) if "z" in done else (zh, zl)
        return weight.at[hd, u, yy, zz, xx, zzl, core]

    def w_push(hd, u, phase, step):
        axes = w_axes(hd, u)
        region = w_region(hd, u, axes[:phase])
        n = ((hd * 2 + u) * 3 + phase) * 3 + step - 1
        return remote(region, region, w_send.at[n], w_recv.at[n], along(axes[phase], step))

    def w_start(hd, phase):
        for u in range(2):
            for step in (1, 2, 3):
                w_push(hd, u, phase, step).start()

    def w_arrived(hd, phase):
        for u in range(2):
            for step in (1, 2, 3):
                w_push(hd, u, phase, step).wait_recv()

    def w_swap(hd, u):
        region = w_region(hd, u, "xyz")
        return remote(region, region, ws_send.at[hd, u], ws_recv.at[hd, u], partner)

    def w_share(hd):
        for u in range(2):
            for step in (1, 2, 3):
                w_push(hd, u, 2, step).wait_recv()
            w_swap(hd, u).start()

    def project(hd):
        for u in range(2):
            w_swap(hd, u).wait_recv()
        features = tok_ref.shape[1]
        key_part = jnp.dot(tok_ref[...], weight[hd, 0].reshape(features, DH), preferred_element_type=f32)
        kv[hd, 0, :, :DH] = (key_part * cos_ref[...] - pltpu.roll(key_part, DH // 2, 1) * sin_ref[...]).astype(bf16)
        kv[hd, 0, :, DH:] = jnp.dot(
            tok_ref[...], weight[hd, 1].reshape(features, DH), preferred_element_type=f32).astype(bf16)
        for i in far:
            @pl.when(chip + i < CHIPS)
            def _():
                kv_push(hd, i).start()

        @pl.when(core == 0)
        def _():
            kv_own(hd).start()

    def kv_push(hd, i):
        return remote(kv.at[hd, 0], kv.at[hd, 2 * i], kv_send.at[hd, i], kv_recv.at[hd, i], chip_at(i))

    def kv_own(hd):
        return remote(kv.at[hd, 0], kv.at[hd, 1], fw_send.at[hd, 0], fw_recv.at[hd, 0], partner)

    def kv_forward(hd, i):
        return remote(kv.at[hd, 2 * i], kv.at[hd, 2 * i + 1 - 2 * core], fw_send.at[hd, i], fw_recv.at[hd, i], partner)

    def swap(hd):
        return remote(odd.at[hd], theirs.at[hd], swap_send.at[hd], swap_recv.at[hd], partner)

    def sum_push(hd, i):
        return remote(even.at[hd, i], landed.at[hd, i], ps_send.at[hd, i], ps_recv.at[hd, i], chip_at(-i))

    def gp_push(hd, i):
        return remote(gp_all.at[hd, 0], gp_all.at[hd, 2 * i], ag_send.at[hd, i], ag_recv.at[hd, i], chip_at(i))

    def gp_forward(hd, i):
        slot = lax.rem(2 * i + 1 - 2 * core + NCTX, NCTX)
        return remote(gp_all.at[hd, 2 * i], gp_all.at[hd, slot], agf_send.at[hd, i], agf_recv.at[hd, i], partner)

    def tok_push(j):
        to = lax.rem(c + j, NCTX)
        return remote(tok_own.at[:, to], tok_t.at[:, :, pl.ds(j * T, T)], a_send.at[j], a_recv.at[j], (dp, to))

    def dw_push(hd, j):
        to = lax.rem(dp + j, NDP)
        return remote(dw.at[hd, to], dw_landed.at[hd, j], dw_send.at[hd, j], dw_recv.at[hd, j], (to, c))

    tok_copy = pltpu.make_async_copy(tok_own.at[:, c], tok_t.at[:, :, pl.ds(0, T)], tok_local)

    def forward_keys(hd):
        for i in far:
            @pl.when(i <= chip)
            def _():
                kv_push(hd, i).wait_recv()
                kv_forward(hd, i).start()

    def await_keys(hd):
        for i in far:
            @pl.when(i <= chip)
            def _():
                kv_forward(hd, i).wait_recv()

        @pl.when(core == 1)
        def _():
            kv_own(hd).wait_recv()

    def add_pair(hd):
        swap(hd).wait_recv()
        own32[...] = even[hd, 0].astype(f32) + theirs[hd, lax.rem(CHIPS - core, CHIPS)].astype(f32)
        for i in far:
            @pl.when(i <= chip)
            def _():
                total = even[hd, i].astype(f32) + theirs[hd, i - core].astype(f32)
                even[hd, i] = total.astype(bf16)
                sum_push(hd, i).start()

    def finish_block(hd):
        for i in far:
            @pl.when(chip + i < CHIPS)
            def _():
                sum_push(hd, i).wait_recv()
                own32[...] += landed[hd, i].astype(f32)
        key_part = own32[:, :DH]
        key_part = (key_part * cos_ref[...] + pltpu.roll(key_part, DH // 2, 1) * sin_ref[...]).astype(bf16)
        value_part = own32[:, DH:].astype(bf16)
        gp_all[hd, 0, :, :DH] = key_part
        gp_all[hd, 0, :, DH:] = value_part
        gp_own[2 * hd] = key_part
        gp_own[2 * hd + 1] = value_part
        for i in far:
            gp_push(hd, i).start()
        gp_forward(hd, 0).start()

    def forward_grads(hd):
        for i in far:
            gp_push(hd, i).wait_recv()
            gp_forward(hd, i).start()

    def weight_grad(hd):
        for i in range(CHIPS):
            gp_forward(hd, i).wait_recv()
        part = jnp.dot(tok_t[...].reshape(-1, keys), gp_all[hd].reshape(keys, 2 * DH), preferred_element_type=f32)
        dw[hd] = part.reshape(dw.shape[1:])
        for j in range(1, NDP):
            dw_push(hd, j).start()

    @pl.when((h == 0) & (t == 0))
    def _():
        meet([(dp, lax.rem(c + j, NCTX)) for j in range(1, NCTX)]
             + [(lax.rem(dp + j, NDP), c) for j in range(1, NDP)]
             + [along(axis, k) for axis in "xyz" for k in (1, 2, 3)])
        for hd in range(KVH):
            for u in range(2):
                first = (u * KVH + hd) * DH
                weight[hd, u, y, zh, x, zl, core] = w_ref[:, first:first + DH]
        for hd in range(KVH):
            w_start(hd, 0)
        w_arrived(0, 0)
        w_start(0, 1)
        rows = tok_own.shape[2]
        for n in range(tok_ref.shape[1] // T):
            turned = tok_ref[:, n*T:(n+1)*T].T
            for m in range(T // rows):
                g = n * (T // rows) + m
                tok_own[g // NCTX, g % NCTX] = turned[m*rows:(m+1)*rows]
        for j in range(1, NCTX):
            @pl.when(j > c)
            def _():
                kv[:, j] = jnp.zeros((KVH, T, 2 * DH), bf16)
        w_arrived(0, 1)
        w_start(0, 2)
        for hd in range(1, KVH):
            w_arrived(hd, 0)
            w_start(hd, 1)
        w_share(0)
        project(0)
        w_arrived(1, 1)
        w_start(1, 2)
        forward_keys(0)

    @pl.when(t == 0)
    def _():
        await_keys(h)
        dk_acc[...] = jnp.zeros_like(dk_acc)
        dv_acc[...] = jnp.zeros_like(dv_acc)
        kt_scr[...] = kv[h, :, :, :DH].reshape(keys, DH).T
        vt_scr[...] = kv[h, :, :, DH:].reshape(keys, DH).T

    qs = jnp.concatenate([q_ref[:, g*DH:(g+1)*DH] for g in range(QHEADS)], axis=0)
    k = kv[h, :, :, :DH].reshape(keys, DH)
    v = kv[h, :, :, DH:].reshape(keys, DH)
    s = lax.dot_general(k, qs, (((1,), (1,)), ((), ())), preferred_element_type=f32)
    top = None
    for j in range(NCTX):
        part = s[j*T:(j+1)*T]
        if j == 0:
            key = lax.broadcasted_iota(jnp.int32, (T, R), 0)
            token = lax.broadcasted_iota(jnp.int32, (T, R), 1) % T
            part = jnp.where(key <= token, part, -jnp.inf)
        else:
            part = jnp.where(j <= c, part, -jnp.inf)
        s_scr[pl.ds(j*T, T), :] = part
        best = jnp.max(part.reshape(T//8, 8, R), axis=0)
        top = best if top is None else jnp.maximum(top, best)
    top = jnp.max(top, axis=0, keepdims=True)

    weights = jnp.exp2((s_scr[...] - top) * (scale * LOG2E))
    total = jnp.sum(jnp.sum(weights.reshape(keys//8, 8, R), axis=0), axis=0, keepdims=True)
    wt_scr[...] = weights.astype(bf16)
    acc = jnp.dot(vt_scr[...], wt_scr[...], preferred_element_type=f32)
    inv = 1.0 / total
    out_t = (acc * inv).astype(bf16).astype(f32)
    do_t = jnp.concatenate([do_ref[:, g*DH:(g+1)*DH].astype(f32).T for g in range(QHEADS)], axis=1)
    dos_t = (do_t * inv).astype(bf16).astype(f32)
    delta = jnp.sum(dos_t * out_t, axis=0, keepdims=True)
    dos = jnp.concatenate([dos_t[:, g*DH:(g+1)*DH].T for g in range(QHEADS)], axis=0).astype(bf16)
    for g in range(QHEADS):
        out_ref[:, g*DH:(g+1)*DH] = out_t[:, g*DH:(g+1)*DH].T.astype(bf16)

    dprobs = lax.dot_general(v, dos, (((1,), (1,)), ((), ())), preferred_element_type=f32)
    wb = wt_scr[...]
    ds = (dprobs - delta).astype(bf16) * wb
    dq = jnp.dot(kt_scr[...], ds, preferred_element_type=f32) * scale
    dk_acc[...] += jnp.dot(ds, qs, preferred_element_type=f32)
    dv_acc[...] += jnp.dot(wb, dos, preferred_element_type=f32)
    for g in range(QHEADS):
        dq_ref[:, g*DH:(g+1)*DH] = dq[:, g*DH:(g+1)*DH].T.astype(bf16)

    step = h * tiles + t

    @pl.when(step == 1)
    def _():
        w_share(1)
        w_arrived(2, 1)
        w_start(2, 2)

    @pl.when(step == 2)
    def _():
        project(1)

    @pl.when(step == 3)
    def _():
        forward_keys(1)
        w_share(2)
        w_arrived(3, 1)
        w_start(3, 2)
        tok_copy.start()
        for j in range(1, NCTX):
            tok_push(j).start()

    @pl.when(step == 4)
    def _():
        project(2)

    @pl.when(step == 5)
    def _():
        w_share(3)

    @pl.when(step == 6)
    def _():
        forward_keys(2)
        project(3)

    @pl.when(step == 9)
    def _():
        forward_keys(3)
        tok_copy.wait()
        for j in range(1, NCTX):
            tok_push(j).wait_recv()

    @pl.when((t == 0) & (h >= 1))
    def _():
        add_pair(h - 1)

    @pl.when((t == 0) & (h >= 2))
    def _():
        forward_grads(h - 2)

    @pl.when((t == 2) & (h >= 1))
    def _():
        finish_block(h - 1)

    @pl.when((t == 2) & (h >= 2))
    def _():
        weight_grad(h - 2)

    @pl.when(t == tiles - 1)
    def _():
        for q in range(CHIPS):
            for parity, ref in ((0, even), (1, odd)):
                rows = pl.ds((2 * q + parity) * T, T)
                ref[h, q, :, :DH] = (dk_acc[rows, :] * scale).astype(bf16)
                ref[h, q, :, DH:] = dv_acc[rows, :].astype(bf16)
        swap(h).start()

    @pl.when((t == tiles - 1) & (h == KVH - 1))
    def _():
        last = KVH - 1
        forward_grads(last - 1)
        add_pair(last)
        weight_grad(last - 1)
        finish_block(last)
        gp = jnp.concatenate([gp_own[2 * hd + u] for hd in range(KVH) for u in range(2)], axis=1)
        block = weight.shape[4] * weight.shape[5] * weight.shape[6] * weight.shape[7]

        def inputs_part(n, carry):
            w = jnp.concatenate([weight[hd, u, n // 2, n % 2].reshape(block, DH)
                                 for hd in range(KVH) for u in range(2)], axis=1)
            gin_ref[:, pl.ds(pl.multiple_of(n * block, block), block)] = lax.dot_general(
                gp, w, (((1,), (1,)), ((), ())), preferred_element_type=f32).astype(bf16)
            return carry

        lax.fori_loop(0, tok_ref.shape[1] // block, inputs_part, 0)
        forward_grads(last)
        weight_grad(last)
        for hd in range(KVH):
            total_w = dw[hd, dp]
            for j in range(1, NDP):
                dw_push(hd, j).wait_recv()
                total_w = total_w + dw_landed[hd, j]
            gw_ref[:, hd*DH:(hd+1)*DH] = total_w[:, :DH]
            gw_ref[:, (KVH+hd)*DH:(KVH+hd+1)*DH] = total_w[:, DH:]
        for hd in range(KVH):
            for u in range(2):
                for phase in range(3):
                    for k in (1, 2, 3):
                        w_push(hd, u, phase, k).wait_send()
                w_swap(hd, u).wait_send()
            for i in far:
                @pl.when(chip + i < CHIPS)
                def _():
                    kv_push(hd, i).wait_send()

                @pl.when(i <= chip)
                def _():
                    kv_forward(hd, i).wait_send()
                    sum_push(hd, i).wait_send()

                gp_push(hd, i).wait_send()

            @pl.when(core == 0)
            def _():
                kv_own(hd).wait_send()

            swap(hd).wait_send()
            for i in range(CHIPS):
                gp_forward(hd, i).wait_send()
            for j in range(1, NDP):
                dw_push(hd, j).wait_send()
        for j in range(1, NCTX):
            tok_push(j).wait_send()


def main(q, do, tokens, weight, cosine, sine):
    tiles = q.shape[1] // DH // KVH // QHEADS
    keys, R = NCTX * T, QHEADS * T
    tile = pl.BlockSpec((T, R), lambda h, t: (0, h * tiles + t))

    def whole(array):
        return pl.BlockSpec(array.shape, lambda h, t: (0, 0))

    features = tokens.shape[1]
    rows, width = weight.shape
    dma = pltpu.SemaphoreType.DMA
    shared = pltpu.VMEM((KVH, CHIPS, T, 2 * DH), bf16)
    return pl.pallas_call(
        functools.partial(main_kernel, tiles),
        grid=(KVH, tiles),
        in_specs=[tile, tile, whole(tokens), whole(weight), whole(cosine), whole(sine)],
        out_specs=[tile, tile,
                   pl.BlockSpec((T, features), lambda h, t: (0, 0)),
                   pl.BlockSpec((rows, width), lambda h, t: (0, 0))],
        out_shape=[jax.ShapeDtypeStruct(q.shape, bf16), jax.ShapeDtypeStruct(q.shape, bf16),
                   jax.ShapeDtypeStruct((T, features), bf16), jax.ShapeDtypeStruct((rows, width), f32)],
        scratch_shapes=[
            pltpu.VMEM((KVH, NCTX, T, 2 * DH), bf16),
            pltpu.VMEM((keys, R), f32), pltpu.VMEM((keys, R), bf16),
            pltpu.VMEM((DH, keys), bf16), pltpu.VMEM((DH, keys), bf16),
            pltpu.VMEM((keys, DH), f32), pltpu.VMEM((keys, DH), f32),
            shared, shared, shared, shared,
            pltpu.VMEM((T, 2 * DH), f32),
            pltpu.VMEM((KVH, NCTX, T, 2 * DH), bf16),
            pltpu.VMEM((2 * KVH, T, DH), bf16),
            pltpu.VMEM((KVH, 2, 4, 2, 4, 2, 2, rows, DH), bf16),
            pltpu.VMEM((NDP, NCTX, rows, T), bf16), pltpu.VMEM((NDP, rows, keys), bf16),
            pltpu.VMEM((KVH, NDP, rows, 2 * DH), f32), pltpu.VMEM((KVH, NDP, rows, 2 * DH), f32),
            dma((KVH * 18,)), dma((KVH * 18,)), dma((KVH, 2)), dma((KVH, 2)), dma,
            dma((KVH, CHIPS)), dma((KVH, CHIPS)), dma((KVH, CHIPS)), dma((KVH, CHIPS)),
            dma((KVH,)), dma((KVH,)), dma((KVH, CHIPS)), dma((KVH, CHIPS)),
            dma((KVH, CHIPS)), dma((KVH, CHIPS)), dma((KVH, CHIPS)), dma((KVH, CHIPS)),
            dma((KVH, NDP)), dma((KVH, NDP)), dma((NCTX,)), dma((NCTX,))],
        compiler_params=pltpu.CompilerParams(
            collective_id=0, has_side_effects=True, vmem_limit_bytes=60 * 2**20),
        name="projection_attention_exchanges",
    )(q, do, tokens, weight, cosine, sine)


def on_device(inputs, queries, grad_output, kv_weight):
    count = inputs.shape[1]
    ctx = lax.axis_index("ctx")
    cosine, sine = rope_tables(ctx * count + jnp.arange(count, dtype=jnp.int32), DH)
    attn_out, grad_query, grad_inputs, grad_weight = main(
        queries[0], grad_output[0], inputs[0], kv_weight,
        jnp.concatenate([cosine, cosine], axis=1), jnp.concatenate([sine, -sine], axis=1))
    return (attn_out[None], grad_query[None], grad_inputs[None], grad_weight)


def solution(mesh):
    tokens = P("dp", "ctx", None)
    rows = P(("dp", "ctx"), None)
    return jax.shard_map(
        on_device, mesh=mesh, in_specs=(tokens, tokens, tokens, rows),
        out_specs=(tokens, tokens, tokens, rows), check_vma=False)
```

time: 201 us -> 176 us (0.88)
  Pallas kernels: 181 us -> 165 us
  matrix products: 4.63 us -> 0 us
  local copies, waits for them, and re-layouts: 10.6 us -> 6.88 us
    pallas_call x1 -> x0, Pallas kernels: 45.4 us -> none  [gather_weight(): pl.pallas_call(gather_weight_kernel, in_specs=[pl.BlockSpec(memory_space=...]
    pallas_call x1, Pallas kernels: 136 us -> 165 us  [main(): pl.pallas_call(functools.partial(main_kernel, tiles), grid=(KVH, tiles),...]
    dot_general x1 -> x0, matrix products: 4.63 us -> none  [on_device(): projected = jnp.dot(tokens, weight, preferred_element_type=f32)]
    unnamed x15 -> x10, local copies, waits for them, and re-layouts: 8.7 us -> 6.88 us
where the time goes in v3:
time: 176 us; the launch traced here: 173 us
  Pallas kernels  165 us (94%)
  local copies, waits for them, and re-layouts  6.88 us (4%)
    pallas_call x1, Pallas kernels, main(): pl.pallas_call(functools.partial(main_kernel, tiles), grid=(KVH, tiles),...  165 us
    unnamed x10, local copies, waits for them, and re-layouts  6.88 us

profile of v3, /device:TPU:0, one launch (start us, length us, event | category | flops | bytes accessed | tf_op | source)
XLA Modules:
  0.0 173.3 jit_solution(9111416257324599752)
XLA Ops:
  0.7 0.3 multiply_sine_fusion
  1.0 0.8 pad_maximum_fusion
  1.7 164.7 %projection_attention_exchanges.1 = (bf16[128,8192]{1,0:T(8,128)(2,1)}, bf16[128,8192]{1,0:T(8,128)(2,1)}, bf16[128,4096]{1,0:T(8,128)(2,1)}, f32[32,1024]{1,0:T(8,128)}) custom-call(bf16[128,8192]{1,0:T(8,128)(2,1)} %bitcast.8, bf16[128,8192]{1,0:T(8,128)(2,1)} %bitcast.9, bf16[128,4096]{1,0:T(8,128)(2,1)} %bitcast.11, bf16[32,1024]{1,0:T(8,128)(2,1)} %w_ref.1, ...), custom_call_target="tpu_custom_call" | custom-call | tf_op jit(solution)/shard_map/projection_attention_exchanges/pallas_call | solution.py:440
  166.4 0.0 copy-start
  166.4 3.2 %copy.12 = bf16[1,128,8192]{2,1,0:T(8,128)(2,1)} copy(bf16[1,128,8192]{2,1,0:T(8,128)(2,1)} %bitcast.7) | data formatting | bytes 4194304
  169.6 0.0 copy-done
  169.7 0.0 copy-start.1
  169.7 1.3 copy.13
  171.0 0.6 copy-done.1
  171.6 0.0 copy-start.2
  171.6 1.0 copy.14
  172.6 0.1 copy-done.2
  172.6 0.7 copy.15
  (2 shorter events, 0.0 us)
Async XLA Ops:
  166.4 3.3 %copy-start = (bf16[128,8192]{1,0:T(8,128)(2,1)S(1)}, bf16[128,8192]{1,0:T(8,128)(2,1)}, u32[]{:S(2)}) copy-start(bf16[128,8192]{1,0:T(8,128)(2,1)} %get-tuple-element.9) | copy-start | bytes 6291460
  169.7 2.0 %copy-start.1 = (bf16[128,4096]{1,0:T(8,128)(2,1)S(1)}, bf16[128,4096]{1,0:T(8,128)(2,1)}, u32[]{:S(2)}) copy-start(bf16[128,4096]{1,0:T(8,128)(2,1)} %get-tuple-element.10) | copy-start | bytes 3145732
  171.6 1.0 copy-start.2

commit v4 on v3

--- a/solution.py
+++ b/solution.py
@@ -12,7 +12,7 @@
 LOG2E = math.log2(math.e)
 ROPE_BASE = 500000.0
 MESH = pl.DeviceIdType.MESH
-NDP, NCTX = 8, 16
+NCTX = 16
 CHIPS = NCTX // 2
 f32, bf16 = jnp.float32, jnp.bfloat16
 
@@ -41,6 +41,8 @@
 
 
 QHEADS = 4
+GROUP = 8
+SPREAD = 16
 KVH = 4
 T = 128
 
@@ -70,7 +72,7 @@
             src_ref=src, dst_ref=dst, send_sem=send, recv_sem=recv, device_id=device, device_id_type=MESH)
 
     def w_axes(hd, u):
-        return ("zyx", "yxz", "xzy")[(2 * hd + u) % 3]
+        return (("zxy", "yzx"), ("xzy", "yxz"))[hd % 2][u]
 
     def along(axis, step):
         if axis == "x":
@@ -144,22 +146,28 @@
     def sum_push(hd, i):
         return remote(even.at[hd, i], landed.at[hd, i], ps_send.at[hd, i], ps_recv.at[hd, i], chip_at(-i))
 
-    def gp_push(hd, i):
-        return remote(gp_all.at[hd, 0], gp_all.at[hd, 2 * i], ag_send.at[hd, i], ag_recv.at[hd, i], chip_at(i))
-
-    def gp_forward(hd, i):
-        slot = lax.rem(2 * i + 1 - 2 * core + NCTX, NCTX)
-        return remote(gp_all.at[hd, 2 * i], gp_all.at[hd, slot], agf_send.at[hd, i], agf_recv.at[hd, i], partner)
+    def gp_push(hd, dy):
+        return remote(gp_all.at[hd, 0], gp_all.at[hd, 2 * dy], ag_send.at[hd, dy], ag_recv.at[hd, dy], along("y", dy))
+
+    def gp_forward(hd, dy):
+        return remote(gp_all.at[hd, 2 * dy], gp_all.at[hd, 2 * dy + 1],
+                      agf_send.at[hd, dy], agf_recv.at[hd, dy], partner)
 
     def tok_push(j):
-        to = lax.rem(c + j, NCTX)
-        return remote(tok_own.at[:, to], tok_t.at[:, :, pl.ds(j * T, T)], a_send.at[j], a_recv.at[j], (dp, to))
+        to_y, to_core = lax.rem(y + j // 2, 4), lax.rem(core + j % 2, 2)
+        return remote(tok_own.at[to_y, :, :, :, to_core], tok_t.at[:, :, :, :, pl.ds(j * T, T)],
+                      a_send.at[j], a_recv.at[j], device_at(to_y, zh, x, zl, to_core))
+
+    def across(j):
+        to = lax.rem(z + j % 4, 4)
+        return to // 2, lax.rem(x + j // 4, 4), lax.rem(to, 2)
 
     def dw_push(hd, j):
-        to = lax.rem(dp + j, NDP)
-        return remote(dw.at[hd, to], dw_landed.at[hd, j], dw_send.at[hd, j], dw_recv.at[hd, j], (to, c))
-
-    tok_copy = pltpu.make_async_copy(tok_own.at[:, c], tok_t.at[:, :, pl.ds(0, T)], tok_local)
+        to_zh, to_x, to_zl = across(j)
+        return remote(dw.at[hd, to_zh, to_x, to_zl], dw_landed.at[hd, j], dw_send.at[hd, j], dw_recv.at[hd, j],
+                      device_at(y, to_zh, to_x, to_zl, core))
+
+    tok_copy = pltpu.make_async_copy(tok_own.at[y, :, :, :, core], tok_t.at[:, :, :, :, pl.ds(0, T)], tok_local)
 
     def forward_keys(hd):
         for i in far:
@@ -201,28 +209,32 @@
         gp_all[hd, 0, :, DH:] = value_part
         gp_own[2 * hd] = key_part
         gp_own[2 * hd + 1] = value_part
-        for i in far:
-            gp_push(hd, i).start()
+        for dy in (1, 2, 3):
+            gp_push(hd, dy).start()
         gp_forward(hd, 0).start()
 
     def forward_grads(hd):
-        for i in far:
-            gp_push(hd, i).wait_recv()
-            gp_forward(hd, i).start()
+        for dy in (1, 3, 2):
+            gp_push(hd, dy).wait_recv()
+            gp_forward(hd, dy).start()
 
     def weight_grad(hd):
-        for i in range(CHIPS):
-            gp_forward(hd, i).wait_recv()
-        part = jnp.dot(tok_t[...].reshape(-1, keys), gp_all[hd].reshape(keys, 2 * DH), preferred_element_type=f32)
-        dw[hd] = part.reshape(dw.shape[1:])
-        for j in range(1, NDP):
+        for dy in range(4):
+            gp_forward(hd, dy).wait_recv()
+        part = jnp.dot(tok_t[...].reshape(-1, GROUP * T), gp_all[hd].reshape(GROUP * T, 2 * DH),
+                       preferred_element_type=f32)
+        dw[hd] = part.reshape(dw.shape[1:]).astype(bf16)
+        for j in range(1, SPREAD):
             dw_push(hd, j).start()
 
     @pl.when((h == 0) & (t == 0))
     def _():
-        meet([(dp, lax.rem(c + j, NCTX)) for j in range(1, NCTX)]
-             + [(lax.rem(dp + j, NDP), c) for j in range(1, NDP)]
-             + [along(axis, k) for axis in "xyz" for k in (1, 2, 3)])
+        peers = [partner] + [along("y", dy) for dy in (1, 2, 3)]
+        peers += [device_at(lax.rem(y + dy, 4), zh, x, zl, 1 - core) for dy in (1, 2, 3)]
+        for j in range(1, SPREAD):
+            to_zh, to_x, to_zl = across(j)
+            peers.append(device_at(y, to_zh, to_x, to_zl, core))
+        meet(peers)
         for hd in range(KVH):
             for u in range(2):
                 first = (u * KVH + hd) * DH
@@ -231,12 +243,12 @@
             w_start(hd, 0)
         w_arrived(0, 0)
         w_start(0, 1)
-        rows = tok_own.shape[2]
+        rows = tok_own.shape[5]
         for n in range(tok_ref.shape[1] // T):
             turned = tok_ref[:, n*T:(n+1)*T].T
             for m in range(T // rows):
                 g = n * (T // rows) + m
-                tok_own[g // NCTX, g % NCTX] = turned[m*rows:(m+1)*rows]
+                tok_own[g // 32, g // 16 % 2, g // 4 % 4, g // 2 % 2, g % 2] = turned[m*rows:(m+1)*rows]
         for j in range(1, NCTX):
             @pl.when(j > c)
             def _():
@@ -319,7 +331,7 @@
         w_arrived(3, 1)
         w_start(3, 2)
         tok_copy.start()
-        for j in range(1, NCTX):
+        for j in range(1, GROUP):
             tok_push(j).start()
 
     @pl.when(step == 4)
@@ -339,7 +351,7 @@
     def _():
         forward_keys(3)
         tok_copy.wait()
-        for j in range(1, NCTX):
+        for j in range(1, GROUP):
             tok_push(j).wait_recv()
 
     @pl.when((t == 0) & (h >= 1))
@@ -388,10 +400,10 @@
         forward_grads(last)
         weight_grad(last)
         for hd in range(KVH):
-            total_w = dw[hd, dp]
-            for j in range(1, NDP):
+            total_w = dw[hd, zh, x, zl].astype(f32)
+            for j in range(1, SPREAD):
                 dw_push(hd, j).wait_recv()
-                total_w = total_w + dw_landed[hd, j]
+                total_w = total_w + dw_landed[hd, j].astype(f32)
             gw_ref[:, hd*DH:(hd+1)*DH] = total_w[:, :DH]
             gw_ref[:, (KVH+hd)*DH:(KVH+hd+1)*DH] = total_w[:, DH:]
         for hd in range(KVH):
@@ -410,18 +422,18 @@
                     kv_forward(hd, i).wait_send()
                     sum_push(hd, i).wait_send()
 
-                gp_push(hd, i).wait_send()
-
             @pl.when(core == 0)
             def _():
                 kv_own(hd).wait_send()
 
             swap(hd).wait_send()
-            for i in range(CHIPS):
-                gp_forward(hd, i).wait_send()
-            for j in range(1, NDP):
+            for dy in range(4):
+                gp_forward(hd, dy).wait_send()
+            for dy in (1, 2, 3):
+                gp_push(hd, dy).wait_send()
+            for j in range(1, SPREAD):
                 dw_push(hd, j).wait_send()
-        for j in range(1, NCTX):
+        for j in range(1, GROUP):
             tok_push(j).wait_send()
 
 
@@ -453,16 +465,16 @@
             pltpu.VMEM((keys, DH), f32), pltpu.VMEM((keys, DH), f32),
             shared, shared, shared, shared,
             pltpu.VMEM((T, 2 * DH), f32),
-            pltpu.VMEM((KVH, NCTX, T, 2 * DH), bf16),
+            pltpu.VMEM((KVH, GROUP, T, 2 * DH), bf16),
             pltpu.VMEM((2 * KVH, T, DH), bf16),
             pltpu.VMEM((KVH, 2, 4, 2, 4, 2, 2, rows, DH), bf16),
-            pltpu.VMEM((NDP, NCTX, rows, T), bf16), pltpu.VMEM((NDP, rows, keys), bf16),
-            pltpu.VMEM((KVH, NDP, rows, 2 * DH), f32), pltpu.VMEM((KVH, NDP, rows, 2 * DH), f32),
+            pltpu.VMEM((4, 2, 4, 2, 2, rows, T), bf16), pltpu.VMEM((2, 4, 2, rows, GROUP * T), bf16),
+            pltpu.VMEM((KVH, 2, 4, 2, rows, 2 * DH), bf16), pltpu.VMEM((KVH, SPREAD, rows, 2 * DH), bf16),
             dma((KVH * 18,)), dma((KVH * 18,)), dma((KVH, 2)), dma((KVH, 2)), dma,
             dma((KVH, CHIPS)), dma((KVH, CHIPS)), dma((KVH, CHIPS)), dma((KVH, CHIPS)),
             dma((KVH,)), dma((KVH,)), dma((KVH, CHIPS)), dma((KVH, CHIPS)),
-            dma((KVH, CHIPS)), dma((KVH, CHIPS)), dma((KVH, CHIPS)), dma((KVH, CHIPS)),
-            dma((KVH, NDP)), dma((KVH, NDP)), dma((NCTX,)), dma((NCTX,))],
+            dma((KVH, 4)), dma((KVH, 4)), dma((KVH, 4)), dma((KVH, 4)),
+            dma((KVH, SPREAD)), dma((KVH, SPREAD)), dma((GROUP,)), dma((GROUP,))],
         compiler_params=pltpu.CompilerParams(
             collective_id=0, has_side_effects=True, vmem_limit_bytes=60 * 2**20),
         name="projection_attention_exchanges",

time: 176 us -> 154 us (0.88)
  Pallas kernels: 165 us -> 144 us
    pallas_call x1, Pallas kernels: 165 us -> 144 us  [main(): pl.pallas_call(functools.partial(main_kernel, tiles), grid=(KVH, tiles),...]
where the time goes in v4:
time: 154 us; the launch traced here: 153 us
  Pallas kernels  144 us (94%)
  local copies, waits for them, and re-layouts  6.88 us (4%)
    pallas_call x1, Pallas kernels, main(): pl.pallas_call(functools.partial(main_kernel, tiles), grid=(KVH, tiles),...  144 us
    unnamed x10, local copies, waits for them, and re-layouts  6.88 us

profile of v4, /device:TPU:0, one launch (start us, length us, event | category | flops | bytes accessed | tf_op | source)
XLA Modules:
  0.0 152.9 jit_solution(10269039240088930351)
XLA Ops:
  0.7 0.3 multiply_sine_fusion
  1.0 0.8 pad_maximum_fusion
  1.7 144.3 %projection_attention_exchanges.1 = (bf16[128,8192]{1,0:T(8,128)(2,1)}, bf16[128,8192]{1,0:T(8,128)(2,1)}, bf16[128,4096]{1,0:T(8,128)(2,1)}, f32[32,1024]{1,0:T(8,128)}) custom-call(bf16[128,8192]{1,0:T(8,128)(2,1)} %bitcast.8, bf16[128,8192]{1,0:T(8,128)(2,1)} %bitcast.9, bf16[128,4096]{1,0:T(8,128)(2,1)} %bitcast.11, bf16[32,1024]{1,0:T(8,128)(2,1)} %w_ref.1, ...), custom_call_target="tpu_custom_call" | custom-call | tf_op jit(solution)/shard_map/projection_attention_exchanges/pallas_call | solution.py:452
  146.0 0.0 copy-start
  146.0 3.2 %copy.12 = bf16[1,128,8192]{2,1,0:T(8,128)(2,1)} copy(bf16[1,128,8192]{2,1,0:T(8,128)(2,1)} %bitcast.7) | data formatting | bytes 4194304
  149.3 0.0 copy-done
  149.3 0.0 copy-start.1
  149.3 1.3 copy.13
  150.6 0.6 copy-done.1
  151.2 0.0 copy-start.2
  151.2 1.0 copy.14
  152.2 0.1 copy-done.2
  152.3 0.7 copy.15
  (2 shorter events, 0.0 us)
Async XLA Ops:
  146.0 3.3 %copy-start = (bf16[128,8192]{1,0:T(8,128)(2,1)S(1)}, bf16[128,8192]{1,0:T(8,128)(2,1)}, u32[]{:S(2)}) copy-start(bf16[128,8192]{1,0:T(8,128)(2,1)} %get-tuple-element.9) | copy-start | bytes 6291460
  149.3 2.0 %copy-start.1 = (bf16[128,4096]{1,0:T(8,128)(2,1)S(1)}, bf16[128,4096]{1,0:T(8,128)(2,1)}, u32[]{:S(2)}) copy-start(bf16[128,4096]{1,0:T(8,128)(2,1)} %get-tuple-element.10) | copy-start | bytes 3145732
  151.2 1.0 copy-start.2

commit v5 on v4

--- a/solution.py
+++ b/solution.py
@@ -40,7 +40,7 @@
     pl.semaphore_wait(barrier, len(peers))
 
 
-QHEADS = 4
+QHEADS = 8
 GROUP = 8
 SPREAD = 16
 KVH = 4
@@ -50,7 +50,7 @@
 def main_kernel(tiles, q_ref, do_ref, tok_ref, w_ref, cos_ref, sin_ref,
                 out_ref, dq_ref, gin_ref, gw_ref,
                 kv, s_scr, wt_scr, kt_scr, vt_scr, dk_acc, dv_acc,
-                even, odd, theirs, landed, own32, gp_all, gp_own, weight, tok_own, tok_t, dw, dw_landed,
+                even, odd, theirs, landed, own32, gp_all, gp_own, weight, tok_own, tok_t, dw, dw_landed, gin_acc,
                 w_send, w_recv, ws_send, ws_recv, tok_local, kv_send, kv_recv, fw_send, fw_recv, swap_send, swap_recv, ps_send, ps_recv,
                 ag_send, ag_recv, agf_send, agf_recv, dw_send, dw_recv, a_send, a_recv):
     dp, c = lax.axis_index("dp"), lax.axis_index("ctx")
@@ -71,8 +71,10 @@
         return pltpu.make_async_remote_copy(
             src_ref=src, dst_ref=dst, send_sem=send, recv_sem=recv, device_id=device, device_id_type=MESH)
 
-    def w_axes(hd, u):
-        return (("zxy", "yzx"), ("xzy", "yxz"))[hd % 2][u]
+    def w_units(hd, u):
+        if hd == 0:
+            return ((0, 16, ("zxy", "xyz")[u]), (16, 16, ("yzx", "zxy")[u]))
+        return ((0, 32, (("zxy", "yzx"), ("xzy", "yxz"))[hd % 2][u]),)
 
     def along(axis, step):
         if axis == "x":
@@ -82,63 +84,70 @@
         to = lax.rem(z + step, 4)
         return device_at(y, to // 2, x, lax.rem(to, 2), core)
 
-    def w_region(hd, u, done):
+    def w_region(hd, u, unit, phase):
+        first, count, axes = unit
+        done = axes[:phase]
         yy = slice(None) if "y" in done else y
         xx = slice(None) if "x" in done else x
         zz, zzl = (slice(None), slice(None)) if "z" in done else (zh, zl)
-        return weight.at[hd, u, yy, zz, xx, zzl, core]
-
-    def w_push(hd, u, phase, step):
-        axes = w_axes(hd, u)
-        region = w_region(hd, u, axes[:phase])
-        n = ((hd * 2 + u) * 3 + phase) * 3 + step - 1
-        return remote(region, region, w_send.at[n], w_recv.at[n], along(axes[phase], step))
-
-    def w_start(hd, phase):
-        for u in range(2):
-            for step in (1, 2, 3):
-                w_push(hd, u, phase, step).start()
-
-    def w_arrived(hd, phase):
-        for u in range(2):
-            for step in (1, 2, 3):
-                w_push(hd, u, phase, step).wait_recv()
-
-    def w_swap(hd, u):
-        region = w_region(hd, u, "xyz")
-        return remote(region, region, ws_send.at[hd, u], ws_recv.at[hd, u], partner)
-
-    def w_share(hd):
-        for u in range(2):
-            for step in (1, 2, 3):
-                w_push(hd, u, 2, step).wait_recv()
-            w_swap(hd, u).start()
-
-    def project(hd):
-        for u in range(2):
-            w_swap(hd, u).wait_recv()
-        features = tok_ref.shape[1]
-        key_part = jnp.dot(tok_ref[...], weight[hd, 0].reshape(features, DH), preferred_element_type=f32)
-        kv[hd, 0, :, :DH] = (key_part * cos_ref[...] - pltpu.roll(key_part, DH // 2, 1) * sin_ref[...]).astype(bf16)
-        kv[hd, 0, :, DH:] = jnp.dot(
-            tok_ref[...], weight[hd, 1].reshape(features, DH), preferred_element_type=f32).astype(bf16)
-        for i in far:
-            @pl.when(chip + i < CHIPS)
+        return weight.at[hd, u, yy, zz, xx, zzl, core, pl.ds(first, count)]
+
+    def w_push(hd, u, unit, phase, step):
+        region = w_region(hd, u, unit, phase)
+        n = (((hd * 2 + u) * 2 + unit[0] // 16) * 3 + phase) * 3 + step - 1
+        return remote(region, region, w_send.at[n], w_recv.at[n], along(unit[2][phase], step))
+
+    def w_start(hd, phase, us=(0, 1)):
+        for u in us:
+            for unit in w_units(hd, u):
+                for step in (2, 1, 3):
+                    w_push(hd, u, unit, phase, step).start()
+
+    def w_arrived(hd, phase, us=(0, 1)):
+        for u in us:
+            for unit in w_units(hd, u):
+                for step in (1, 3, 2):
+                    w_push(hd, u, unit, phase, step).wait_recv()
+
+    def w_swap(hd, u, unit):
+        region = w_region(hd, u, unit, 3)
+        n = (hd * 2 + u) * 2 + unit[0] // 16
+        return remote(region, region, ws_send.at[n], ws_recv.at[n], partner)
+
+    def w_share(hd, us=(0, 1)):
+        for u in us:
+            for unit in w_units(hd, u):
+                for step in (1, 3, 2):
+                    w_push(hd, u, unit, 2, step).wait_recv()
+                w_swap(hd, u, unit).start()
+
+    def project(hd, us=(0, 1)):
+        for u in us:
+            for unit in w_units(hd, u):
+                w_swap(hd, u, unit).wait_recv()
+            part = jnp.dot(tok_ref[...], weight[hd, u].reshape(tok_ref.shape[1], DH), preferred_element_type=f32)
+            if u == 0:
+                part = part * cos_ref[...] - pltpu.roll(part, DH // 2, 1) * sin_ref[...]
+            kv[hd, u, 0] = part.astype(bf16)
+            for i in far:
+                @pl.when(chip + i < CHIPS)
+                def _():
+                    kv_push(hd, u, i).start()
+
+            @pl.when(core == 0)
             def _():
-                kv_push(hd, i).start()
-
-        @pl.when(core == 0)
-        def _():
-            kv_own(hd).start()
-
-    def kv_push(hd, i):
-        return remote(kv.at[hd, 0], kv.at[hd, 2 * i], kv_send.at[hd, i], kv_recv.at[hd, i], chip_at(i))
-
-    def kv_own(hd):
-        return remote(kv.at[hd, 0], kv.at[hd, 1], fw_send.at[hd, 0], fw_recv.at[hd, 0], partner)
-
-    def kv_forward(hd, i):
-        return remote(kv.at[hd, 2 * i], kv.at[hd, 2 * i + 1 - 2 * core], fw_send.at[hd, i], fw_recv.at[hd, i], partner)
+                kv_own(hd, u).start()
+
+    def kv_push(hd, u, i):
+        return remote(kv.at[hd, u, 0], kv.at[hd, u, 2 * i],
+                      kv_send.at[hd, u, i], kv_recv.at[hd, u, i], chip_at(i))
+
+    def kv_own(hd, u):
+        return remote(kv.at[hd, u, 0], kv.at[hd, u, 1], fw_send.at[hd, u, 0], fw_recv.at[hd, u, 0], partner)
+
+    def kv_forward(hd, u, i):
+        return remote(kv.at[hd, u, 2 * i], kv.at[hd, u, 2 * i + 1 - 2 * core],
+                      fw_send.at[hd, u, i], fw_recv.at[hd, u, i], partner)
 
     def swap(hd):
         return remote(odd.at[hd], theirs.at[hd], swap_send.at[hd], swap_recv.at[hd], partner)
@@ -169,22 +178,23 @@
 
     tok_copy = pltpu.make_async_copy(tok_own.at[y, :, :, :, core], tok_t.at[:, :, :, :, pl.ds(0, T)], tok_local)
 
-    def forward_keys(hd):
+    def forward_keys(hd, us=(0, 1)):
+        for u in us:
+            for i in far:
+                @pl.when(i <= chip)
+                def _():
+                    kv_push(hd, u, i).wait_recv()
+                    kv_forward(hd, u, i).start()
+
+    def await_keys(hd, u):
         for i in far:
             @pl.when(i <= chip)
             def _():
-                kv_push(hd, i).wait_recv()
-                kv_forward(hd, i).start()
-
-    def await_keys(hd):
-        for i in far:
-            @pl.when(i <= chip)
-            def _():
-                kv_forward(hd, i).wait_recv()
+                kv_forward(hd, u, i).wait_recv()
 
         @pl.when(core == 1)
         def _():
-            kv_own(hd).wait_recv()
+            kv_own(hd, u).wait_recv()
 
     def add_pair(hd):
         swap(hd).wait_recv()
@@ -239,42 +249,45 @@
             for u in range(2):
                 first = (u * KVH + hd) * DH
                 weight[hd, u, y, zh, x, zl, core] = w_ref[:, first:first + DH]
-        for hd in range(KVH):
+        for u in range(2):
+            w_start(0, 0, (u,))
+        for phase in range(2):
+            for u in range(2):
+                w_arrived(0, phase, (u,))
+                w_start(0, phase + 1, (u,))
+        for hd in range(1, KVH):
             w_start(hd, 0)
-        w_arrived(0, 0)
-        w_start(0, 1)
         rows = tok_own.shape[5]
         for n in range(tok_ref.shape[1] // T):
             turned = tok_ref[:, n*T:(n+1)*T].T
             for m in range(T // rows):
                 g = n * (T // rows) + m
                 tok_own[g // 32, g // 16 % 2, g // 4 % 4, g // 2 % 2, g % 2] = turned[m*rows:(m+1)*rows]
+        w_share(0, (0,))
+        w_share(0, (1,))
+        project(0, (0,))
+        project(0, (1,))
+        for hd in range(1, KVH):
+            w_arrived(hd, 0)
+            w_start(hd, 1)
         for j in range(1, NCTX):
             @pl.when(j > c)
             def _():
-                kv[:, j] = jnp.zeros((KVH, T, 2 * DH), bf16)
-        w_arrived(0, 1)
-        w_start(0, 2)
-        for hd in range(1, KVH):
-            w_arrived(hd, 0)
-            w_start(hd, 1)
-        w_share(0)
-        project(0)
+                kv[:, :, j] = jnp.zeros((KVH, 2, T, DH), bf16)
+        forward_keys(0, (0,))
         w_arrived(1, 1)
         w_start(1, 2)
-        forward_keys(0)
+        forward_keys(0, (1,))
 
     @pl.when(t == 0)
     def _():
-        await_keys(h)
+        await_keys(h, 0)
         dk_acc[...] = jnp.zeros_like(dk_acc)
         dv_acc[...] = jnp.zeros_like(dv_acc)
-        kt_scr[...] = kv[h, :, :, :DH].reshape(keys, DH).T
-        vt_scr[...] = kv[h, :, :, DH:].reshape(keys, DH).T
+        kt_scr[...] = kv[h, 0].reshape(keys, DH).T
 
     qs = jnp.concatenate([q_ref[:, g*DH:(g+1)*DH] for g in range(QHEADS)], axis=0)
-    k = kv[h, :, :, :DH].reshape(keys, DH)
-    v = kv[h, :, :, DH:].reshape(keys, DH)
+    k = kv[h, 0].reshape(keys, DH)
     s = lax.dot_general(k, qs, (((1,), (1,)), ((), ())), preferred_element_type=f32)
     top = None
     for j in range(NCTX):
@@ -290,6 +303,11 @@
         top = best if top is None else jnp.maximum(top, best)
     top = jnp.max(top, axis=0, keepdims=True)
 
+    @pl.when(t == 0)
+    def _():
+        await_keys(h, 1)
+        vt_scr[...] = kv[h, 1].reshape(keys, DH).T
+
     weights = jnp.exp2((s_scr[...] - top) * (scale * LOG2E))
     total = jnp.sum(jnp.sum(weights.reshape(keys//8, 8, R), axis=0), axis=0, keepdims=True)
     wt_scr[...] = weights.astype(bf16)
@@ -303,7 +321,38 @@
     for g in range(QHEADS):
         out_ref[:, g*DH:(g+1)*DH] = out_t[:, g*DH:(g+1)*DH].T.astype(bf16)
 
-    dprobs = lax.dot_general(v, dos, (((1,), (1,)), ((), ())), preferred_element_type=f32)
+    step = h * tiles + t
+
+    @pl.when(step == 1)
+    def _():
+        project(1)
+
+    @pl.when((t == 0) & (h >= 1))
+    def _():
+        add_pair(h - 1)
+
+    @pl.when(step == 2)
+    def _():
+        project(2)
+
+    @pl.when(step == 3)
+    def _():
+        forward_keys(2)
+        project(3)
+
+    @pl.when((t == 0) & (h >= 2))
+    def _():
+        forward_grads(h - 2)
+
+    @pl.when((t == 1) & (h >= 1))
+    def _():
+        finish_block(h - 1)
+
+    @pl.when((t == 1) & (h >= 2))
+    def _():
+        weight_grad(h - 2)
+
+    dprobs = lax.dot_general(kv[h, 1].reshape(keys, DH), dos, (((1,), (1,)), ((), ())), preferred_element_type=f32)
     wb = wt_scr[...]
     ds = (dprobs - delta).astype(bf16) * wb
     dq = jnp.dot(kt_scr[...], ds, preferred_element_type=f32) * scale
@@ -312,19 +361,13 @@
     for g in range(QHEADS):
         dq_ref[:, g*DH:(g+1)*DH] = dq[:, g*DH:(g+1)*DH].T.astype(bf16)
 
-    step = h * tiles + t
-
-    @pl.when(step == 1)
+    @pl.when(step == 0)
     def _():
         w_share(1)
         w_arrived(2, 1)
         w_start(2, 2)
 
-    @pl.when(step == 2)
-    def _():
-        project(1)
-
-    @pl.when(step == 3)
+    @pl.when(step == 1)
     def _():
         forward_keys(1)
         w_share(2)
@@ -334,41 +377,16 @@
         for j in range(1, GROUP):
             tok_push(j).start()
 
+    @pl.when(step == 2)
+    def _():
+        w_share(3)
+
     @pl.when(step == 4)
-    def _():
-        project(2)
-
-    @pl.when(step == 5)
-    def _():
-        w_share(3)
-
-    @pl.when(step == 6)
-    def _():
-        forward_keys(2)
-        project(3)
-
-    @pl.when(step == 9)
     def _():
         forward_keys(3)
         tok_copy.wait()
         for j in range(1, GROUP):
             tok_push(j).wait_recv()
-
-    @pl.when((t == 0) & (h >= 1))
-    def _():
-        add_pair(h - 1)
-
-    @pl.when((t == 0) & (h >= 2))
-    def _():
-        forward_grads(h - 2)
-
-    @pl.when((t == 2) & (h >= 1))
-    def _():
-        finish_block(h - 1)
-
-    @pl.when((t == 2) & (h >= 2))
-    def _():
-        weight_grad(h - 2)
 
     @pl.when(t == tiles - 1)
     def _():
@@ -385,18 +403,21 @@
         forward_grads(last - 1)
         add_pair(last)
         weight_grad(last - 1)
+        block = weight.shape[4] * weight.shape[5] * weight.shape[6] * weight.shape[7]
+
+        def inputs_part(heads):
+            gp = jnp.concatenate([gp_own[2 * hd + u] for hd in heads for u in range(2)], axis=1)
+            for n in range(tok_ref.shape[1] // block):
+                w = jnp.concatenate([weight[hd, u, n // 2, n % 2].reshape(block, DH)
+                                     for hd in heads for u in range(2)], axis=1)
+                yield slice(n * block, (n + 1) * block), lax.dot_general(
+                    gp, w, (((1,), (1,)), ((), ())), preferred_element_type=f32)
+
+        for columns, part in inputs_part(range(last)):
+            gin_acc[:, columns] = part
         finish_block(last)
-        gp = jnp.concatenate([gp_own[2 * hd + u] for hd in range(KVH) for u in range(2)], axis=1)
-        block = weight.shape[4] * weight.shape[5] * weight.shape[6] * weight.shape[7]
-
-        def inputs_part(n, carry):
-            w = jnp.concatenate([weight[hd, u, n // 2, n % 2].reshape(block, DH)
-                                 for hd in range(KVH) for u in range(2)], axis=1)
-            gin_ref[:, pl.ds(pl.multiple_of(n * block, block), block)] = lax.dot_general(
-                gp, w, (((1,), (1,)), ((), ())), preferred_element_type=f32).astype(bf16)
-            return carry
-
-        lax.fori_loop(0, tok_ref.shape[1] // block, inputs_part, 0)
+        for columns, part in inputs_part([last]):
+            gin_ref[:, columns] = (gin_acc[:, columns] + part).astype(bf16)
         forward_grads(last)
         weight_grad(last)
         for hd in range(KVH):
@@ -408,23 +429,27 @@
             gw_ref[:, (KVH+hd)*DH:(KVH+hd+1)*DH] = total_w[:, DH:]
         for hd in range(KVH):
             for u in range(2):
-                for phase in range(3):
-                    for k in (1, 2, 3):
-                        w_push(hd, u, phase, k).wait_send()
-                w_swap(hd, u).wait_send()
+                for unit in w_units(hd, u):
+                    for phase in range(3):
+                        for k in (1, 2, 3):
+                            w_push(hd, u, unit, phase, k).wait_send()
+                    w_swap(hd, u, unit).wait_send()
             for i in far:
                 @pl.when(chip + i < CHIPS)
                 def _():
-                    kv_push(hd, i).wait_send()
+                    for u in range(2):
+                        kv_push(hd, u, i).wait_send()
 
                 @pl.when(i <= chip)
                 def _():
-                    kv_forward(hd, i).wait_send()
+                    for u in range(2):
+                        kv_forward(hd, u, i).wait_send()
                     sum_push(hd, i).wait_send()
 
             @pl.when(core == 0)
             def _():
-                kv_own(hd).wait_send()
+                for u in range(2):
+                    kv_own(hd, u).wait_send()
 
             swap(hd).wait_send()
             for dy in range(4):
@@ -459,7 +484,7 @@
         out_shape=[jax.ShapeDtypeStruct(q.shape, bf16), jax.ShapeDtypeStruct(q.shape, bf16),
                    jax.ShapeDtypeStruct((T, features), bf16), jax.ShapeDtypeStruct((rows, width), f32)],
         scratch_shapes=[
-            pltpu.VMEM((KVH, NCTX, T, 2 * DH), bf16),
+            pltpu.VMEM((KVH, 2, NCTX, T, DH), bf16),
             pltpu.VMEM((keys, R), f32), pltpu.VMEM((keys, R), bf16),
             pltpu.VMEM((DH, keys), bf16), pltpu.VMEM((DH, keys), bf16),
             pltpu.VMEM((keys, DH), f32), pltpu.VMEM((keys, DH), f32),
@@ -470,8 +495,9 @@
             pltpu.VMEM((KVH, 2, 4, 2, 4, 2, 2, rows, DH), bf16),
             pltpu.VMEM((4, 2, 4, 2, 2, rows, T), bf16), pltpu.VMEM((2, 4, 2, rows, GROUP * T), bf16),
             pltpu.VMEM((KVH, 2, 4, 2, rows, 2 * DH), bf16), pltpu.VMEM((KVH, SPREAD, rows, 2 * DH), bf16),
-            dma((KVH * 18,)), dma((KVH * 18,)), dma((KVH, 2)), dma((KVH, 2)), dma,
-            dma((KVH, CHIPS)), dma((KVH, CHIPS)), dma((KVH, CHIPS)), dma((KVH, CHIPS)),
+            pltpu.VMEM((T, features), f32),
+            dma((KVH * 36,)), dma((KVH * 36,)), dma((KVH * 4,)), dma((KVH * 4,)), dma,
+            dma((KVH, 2, CHIPS)), dma((KVH, 2, CHIPS)), dma((KVH, 2, CHIPS)), dma((KVH, 2, CHIPS)),
             dma((KVH,)), dma((KVH,)), dma((KVH, CHIPS)), dma((KVH, CHIPS)),
             dma((KVH, 4)), dma((KVH, 4)), dma((KVH, 4)), dma((KVH, 4)),
             dma((KVH, SPREAD)), dma((KVH, SPREAD)), dma((GROUP,)), dma((GROUP,))],

time: 154 us -> 149 us (0.968)
  Pallas kernels: 144 us -> 140 us
    pallas_call x1, Pallas kernels: 144 us -> 140 us  [main(): pl.pallas_call(functools.partial(main_kernel, tiles), grid=(KVH, tiles),...]
where the time goes in v5:
time: 149 us
  Pallas kernels  140 us (94%)
  local copies, waits for them, and re-layouts  6.88 us (5%)
    pallas_call x1, Pallas kernels, main(): pl.pallas_call(functools.partial(main_kernel, tiles), grid=(KVH, tiles),...  140 us
    unnamed x10, local copies, waits for them, and re-layouts  6.88 us

profile of v5, /device:TPU:0, one launch (start us, length us, event | category | flops | bytes accessed | tf_op | source)
XLA Modules:
  0.0 148.9 jit_solution(3608992733737011392)
XLA Ops:
  0.7 0.3 multiply_sine_fusion
  1.0 0.8 pad_maximum_fusion
  1.7 140.3 %projection_attention_exchanges.1 = (bf16[128,8192]{1,0:T(8,128)(2,1)}, bf16[128,8192]{1,0:T(8,128)(2,1)}, bf16[128,4096]{1,0:T(8,128)(2,1)}, f32[32,1024]{1,0:T(8,128)}) custom-call(bf16[128,8192]{1,0:T(8,128)(2,1)} %bitcast.8, bf16[128,8192]{1,0:T(8,128)(2,1)} %bitcast.9, bf16[128,4096]{1,0:T(8,128)(2,1)} %bitcast.11, bf16[32,1024]{1,0:T(8,128)(2,1)} %w_ref.1, ...), custom_call_target="tpu_custom_call" | custom-call | tf_op jit(solution)/shard_map/projection_attention_exchanges/pallas_call | solution.py:477
  142.0 0.0 copy-start
  142.0 3.2 %copy.12 = bf16[1,128,8192]{2,1,0:T(8,128)(2,1)} copy(bf16[1,128,8192]{2,1,0:T(8,128)(2,1)} %bitcast.7) | data formatting | bytes 4194304
  145.3 0.0 copy-done
  145.3 0.0 copy-start.1
  145.3 1.3 copy.13
  146.6 0.6 copy-done.1
  147.3 0.0 copy-start.2
  147.3 1.0 copy.14
  148.2 0.1 copy-done.2
  148.3 0.7 copy.15
  (2 shorter events, 0.0 us)
Async XLA Ops:
  142.0 3.3 %copy-start = (bf16[128,8192]{1,0:T(8,128)(2,1)S(1)}, bf16[128,8192]{1,0:T(8,128)(2,1)}, u32[]{:S(2)}) copy-start(bf16[128,8192]{1,0:T(8,128)(2,1)} %get-tuple-element.9) | copy-start | bytes 6291460
  145.3 2.0 %copy-start.1 = (bf16[128,4096]{1,0:T(8,128)(2,1)S(1)}, bf16[128,4096]{1,0:T(8,128)(2,1)}, u32[]{:S(2)}) copy-start(bf16[128,4096]{1,0:T(8,128)(2,1)} %get-tuple-element.10) | copy-start | bytes 3145732
  147.3 1.0 copy-start.2

commit v6 on v5

--- a/solution.py
+++ b/solution.py
@@ -92,10 +92,20 @@
         zz, zzl = (slice(None), slice(None)) if "z" in done else (zh, zl)
         return weight.at[hd, u, yy, zz, xx, zzl, core, pl.ds(first, count)]
 
+    def w_number(hd, u, unit):
+        return 2 * u + unit[0] // 16 if hd == 0 else 2 + 2 * hd + u
+
     def w_push(hd, u, unit, phase, step):
         region = w_region(hd, u, unit, phase)
-        n = (((hd * 2 + u) * 2 + unit[0] // 16) * 3 + phase) * 3 + step - 1
+        n = w_number(hd, u, unit) * 3 + phase
         return remote(region, region, w_send.at[n], w_recv.at[n], along(unit[2][phase], step))
+
+    def w_three(hd, u, unit, phase):
+        first, count, _ = unit
+        rest = ((0, 0, 0), (0, slice(None), 0), (slice(None), slice(None), slice(None)))[phase]
+        region = weight.at[(hd, u, pl.ds(0, 3)) + rest + (core, pl.ds(first, count))]
+        n = w_number(hd, u, unit) * 3 + phase
+        return remote(region, region, w_send.at[n], w_recv.at[n], partner)
 
     def w_start(hd, phase, us=(0, 1)):
         for u in us:
@@ -106,19 +116,17 @@
     def w_arrived(hd, phase, us=(0, 1)):
         for u in us:
             for unit in w_units(hd, u):
-                for step in (1, 3, 2):
-                    w_push(hd, u, unit, phase, step).wait_recv()
+                w_three(hd, u, unit, phase).wait_recv()
 
     def w_swap(hd, u, unit):
         region = w_region(hd, u, unit, 3)
-        n = (hd * 2 + u) * 2 + unit[0] // 16
+        n = w_number(hd, u, unit)
         return remote(region, region, ws_send.at[n], ws_recv.at[n], partner)
 
     def w_share(hd, us=(0, 1)):
         for u in us:
             for unit in w_units(hd, u):
-                for step in (1, 3, 2):
-                    w_push(hd, u, unit, 2, step).wait_recv()
+                w_three(hd, u, unit, 2).wait_recv()
                 w_swap(hd, u, unit).start()
 
     def project(hd, us=(0, 1)):
@@ -128,44 +136,67 @@
             part = jnp.dot(tok_ref[...], weight[hd, u].reshape(tok_ref.shape[1], DH), preferred_element_type=f32)
             if u == 0:
                 part = part * cos_ref[...] - pltpu.roll(part, DH // 2, 1) * sin_ref[...]
-            kv[hd, u, 0] = part.astype(bf16)
-            for i in far:
-                @pl.when(chip + i < CHIPS)
-                def _():
-                    kv_push(hd, u, i).start()
-
-            @pl.when(core == 0)
-            def _():
-                kv_own(hd, u).start()
-
-    def kv_push(hd, u, i):
-        return remote(kv.at[hd, u, 0], kv.at[hd, u, 2 * i],
-                      kv_send.at[hd, u, i], kv_recv.at[hd, u, i], chip_at(i))
-
-    def kv_own(hd, u):
-        return remote(kv.at[hd, u, 0], kv.at[hd, u, 1], fw_send.at[hd, u, 0], fw_recv.at[hd, u, 0], partner)
-
-    def kv_forward(hd, u, i):
-        return remote(kv.at[hd, u, 2 * i], kv.at[hd, u, 2 * i + 1 - 2 * core],
-                      fw_send.at[hd, u, i], fw_recv.at[hd, u, i], partner)
+            kv[hd, u, 0, 0] = part.astype(bf16)
+        for i in far:
+            @pl.when(chip + i < CHIPS)
+            def _():
+                kv_push(hd, us, i).start()
+
+    def wait_for(n, stand_in, way):
+        for count in far:
+            @pl.when(n == count)
+            def _():
+                getattr(stand_in(count), way)()
+
+    def kv_part(hd, us):
+        return hd + 1 if len(us) == 2 else us[0]
+
+    def kv_at(hd, us, parity, slots):
+        return kv.at[hd, pl.ds(us[0], len(us)), parity, slots]
+
+    def kv_push(hd, us, i):
+        n = kv_part(hd, us)
+        return remote(kv_at(hd, us, 0, 0), kv_at(hd, us, 0, i), kv_send.at[n], kv_recv.at[n], chip_at(i))
+
+    def kv_some(hd, us, count):
+        n = kv_part(hd, us)
+        region = kv_at(hd, us, 0, pl.ds(1, count))
+        return remote(region, region, kv_send.at[n], kv_recv.at[n], partner)
+
+    def kv_forward(hd, us, from_core):
+        n = kv_part(hd, us)
+        here, there = (pl.ds(0, 8), pl.ds(0, 8)) if from_core == 0 else (pl.ds(1, 7), pl.ds(0, 7))
+        return remote(kv_at(hd, us, 0, here), kv_at(hd, us, 1, there), fw_send.at[n], fw_recv.at[n], partner)
 
     def swap(hd):
         return remote(odd.at[hd], theirs.at[hd], swap_send.at[hd], swap_recv.at[hd], partner)
 
     def sum_push(hd, i):
-        return remote(even.at[hd, i], landed.at[hd, i], ps_send.at[hd, i], ps_recv.at[hd, i], chip_at(-i))
+        return remote(even.at[hd, i], landed.at[hd, i], ps_send.at[hd], ps_recv.at[hd], chip_at(-i))
+
+    def sum_some(hd, count):
+        region = landed.at[hd, pl.ds(1, count)]
+        return remote(region, region, ps_send.at[hd], ps_recv.at[hd], partner)
 
     def gp_push(hd, dy):
-        return remote(gp_all.at[hd, 0], gp_all.at[hd, 2 * dy], ag_send.at[hd, dy], ag_recv.at[hd, dy], along("y", dy))
-
-    def gp_forward(hd, dy):
-        return remote(gp_all.at[hd, 2 * dy], gp_all.at[hd, 2 * dy + 1],
-                      agf_send.at[hd, dy], agf_recv.at[hd, dy], partner)
+        return remote(gp_all.at[hd, 0], gp_all.at[hd, dy], ag_send.at[hd], ag_recv.at[hd], along("y", dy))
+
+    def gp_three(hd):
+        region = gp_all.at[hd, pl.ds(1, 3)]
+        return remote(region, region, ag_send.at[hd], ag_recv.at[hd], partner)
+
+    def gp_forward(hd):
+        return remote(gp_all.at[hd, pl.ds(0, 4)], gp_all.at[hd, pl.ds(4, 4)],
+                      agf_send.at[hd], agf_recv.at[hd], partner)
 
     def tok_push(j):
-        to_y, to_core = lax.rem(y + j // 2, 4), lax.rem(core + j % 2, 2)
+        to_y, to_core = lax.rem(y + j % 4, 4), lax.rem(core + j // 4, 2)
         return remote(tok_own.at[to_y, :, :, :, to_core], tok_t.at[:, :, :, :, pl.ds(j * T, T)],
-                      a_send.at[j], a_recv.at[j], device_at(to_y, zh, x, zl, to_core))
+                      a_send, a_recv, device_at(to_y, zh, x, zl, to_core))
+
+    def tok_all():
+        region = tok_t.at[:, :, :, :, pl.ds(T, (GROUP - 1) * T)]
+        return remote(region, region, a_send, a_recv, partner)
 
     def across(j):
         to = lax.rem(z + j % 4, 4)
@@ -173,28 +204,27 @@
 
     def dw_push(hd, j):
         to_zh, to_x, to_zl = across(j)
-        return remote(dw.at[hd, to_zh, to_x, to_zl], dw_landed.at[hd, j], dw_send.at[hd, j], dw_recv.at[hd, j],
+        return remote(dw.at[hd, to_zh, to_x, to_zl], dw_landed.at[hd, j], dw_send.at[hd], dw_recv.at[hd],
                       device_at(y, to_zh, to_x, to_zl, core))
 
+    def dw_all(hd):
+        region = dw_landed.at[hd, pl.ds(1, SPREAD - 1)]
+        return remote(region, region, dw_send.at[hd], dw_recv.at[hd], partner)
+
     tok_copy = pltpu.make_async_copy(tok_own.at[y, :, :, :, core], tok_t.at[:, :, :, :, pl.ds(0, T)], tok_local)
 
     def forward_keys(hd, us=(0, 1)):
-        for u in us:
-            for i in far:
-                @pl.when(i <= chip)
-                def _():
-                    kv_push(hd, u, i).wait_recv()
-                    kv_forward(hd, u, i).start()
-
-    def await_keys(hd, u):
-        for i in far:
-            @pl.when(i <= chip)
-            def _():
-                kv_forward(hd, u, i).wait_recv()
-
-        @pl.when(core == 1)
-        def _():
-            kv_own(hd, u).wait_recv()
+        wait_for(chip, lambda count: kv_some(hd, us, count), "wait_recv")
+        for k in range(2):
+            @pl.when(core == k)
+            def _():
+                kv_forward(hd, us, k).start()
+
+    def await_keys(hd, us):
+        for k in range(2):
+            @pl.when(core == k)
+            def _():
+                kv_forward(hd, us, 1 - k).wait_recv()
 
     def add_pair(hd):
         swap(hd).wait_recv()
@@ -207,10 +237,10 @@
                 sum_push(hd, i).start()
 
     def finish_block(hd):
+        wait_for(CHIPS - 1 - chip, lambda count: sum_some(hd, count), "wait_recv")
         for i in far:
             @pl.when(chip + i < CHIPS)
             def _():
-                sum_push(hd, i).wait_recv()
                 own32[...] += landed[hd, i].astype(f32)
         key_part = own32[:, :DH]
         key_part = (key_part * cos_ref[...] + pltpu.roll(key_part, DH // 2, 1) * sin_ref[...]).astype(bf16)
@@ -221,30 +251,24 @@
         gp_own[2 * hd + 1] = value_part
         for dy in (1, 2, 3):
             gp_push(hd, dy).start()
-        gp_forward(hd, 0).start()
 
     def forward_grads(hd):
-        for dy in (1, 3, 2):
-            gp_push(hd, dy).wait_recv()
-            gp_forward(hd, dy).start()
+        gp_three(hd).wait_recv()
+        gp_forward(hd).start()
 
     def weight_grad(hd):
-        for dy in range(4):
-            gp_forward(hd, dy).wait_recv()
+        gp_forward(hd).wait_recv()
         part = jnp.dot(tok_t[...].reshape(-1, GROUP * T), gp_all[hd].reshape(GROUP * T, 2 * DH),
                        preferred_element_type=f32)
         dw[hd] = part.reshape(dw.shape[1:]).astype(bf16)
         for j in range(1, SPREAD):
             dw_push(hd, j).start()
 
+    step = h * tiles + t
+
     @pl.when((h == 0) & (t == 0))
     def _():
-        peers = [partner] + [along("y", dy) for dy in (1, 2, 3)]
-        peers += [device_at(lax.rem(y + dy, 4), zh, x, zl, 1 - core) for dy in (1, 2, 3)]
-        for j in range(1, SPREAD):
-            to_zh, to_x, to_zl = across(j)
-            peers.append(device_at(y, to_zh, to_x, to_zl, core))
-        meet(peers)
+        meet([partner] + [along(axis, k) for axis in "xyz" for k in (1, 2, 3)])
         for hd in range(KVH):
             for u in range(2):
                 first = (u * KVH + hd) * DH
@@ -270,10 +294,15 @@
         for hd in range(1, KVH):
             w_arrived(hd, 0)
             w_start(hd, 1)
-        for j in range(1, NCTX):
-            @pl.when(j > c)
-            def _():
-                kv[:, :, j] = jnp.zeros((KVH, 2, T, DH), bf16)
+        for i in far:
+            @pl.when(i > chip)
+            def _():
+                kv[:, :, 0, i] = jnp.zeros((KVH, 2, T, DH), bf16)
+
+        @pl.when(core == 0)
+        def _():
+            kv[:, :, 1, CHIPS - 1] = jnp.zeros((KVH, 2, T, DH), bf16)
+
         forward_keys(0, (0,))
         w_arrived(1, 1)
         w_start(1, 2)
@@ -281,7 +310,14 @@
 
     @pl.when(t == 0)
     def _():
-        await_keys(h, 0)
+        @pl.when(h == 0)
+        def _():
+            await_keys(0, (0,))
+
+        @pl.when(h > 0)
+        def _():
+            await_keys(h, (0, 1))
+
         dk_acc[...] = jnp.zeros_like(dk_acc)
         dv_acc[...] = jnp.zeros_like(dv_acc)
         kt_scr[...] = kv[h, 0].reshape(keys, DH).T
@@ -290,22 +326,26 @@
     k = kv[h, 0].reshape(keys, DH)
     s = lax.dot_general(k, qs, (((1,), (1,)), ((), ())), preferred_element_type=f32)
     top = None
-    for j in range(NCTX):
-        part = s[j*T:(j+1)*T]
+    for n in range(NCTX):
+        j = 2 * (n % CHIPS) + n // CHIPS
+        part = s[n*T:(n+1)*T]
         if j == 0:
             key = lax.broadcasted_iota(jnp.int32, (T, R), 0)
             token = lax.broadcasted_iota(jnp.int32, (T, R), 1) % T
             part = jnp.where(key <= token, part, -jnp.inf)
         else:
             part = jnp.where(j <= c, part, -jnp.inf)
-        s_scr[pl.ds(j*T, T), :] = part
+        s_scr[pl.ds(n*T, T), :] = part
         best = jnp.max(part.reshape(T//8, 8, R), axis=0)
         top = best if top is None else jnp.maximum(top, best)
     top = jnp.max(top, axis=0, keepdims=True)
 
+    @pl.when(step == 0)
+    def _():
+        await_keys(0, (1,))
+
     @pl.when(t == 0)
     def _():
-        await_keys(h, 1)
         vt_scr[...] = kv[h, 1].reshape(keys, DH).T
 
     weights = jnp.exp2((s_scr[...] - top) * (scale * LOG2E))
@@ -321,7 +361,6 @@
     for g in range(QHEADS):
         out_ref[:, g*DH:(g+1)*DH] = out_t[:, g*DH:(g+1)*DH].T.astype(bf16)
 
-    step = h * tiles + t
 
     @pl.when(step == 1)
     def _():
@@ -385,14 +424,13 @@
     def _():
         forward_keys(3)
         tok_copy.wait()
-        for j in range(1, GROUP):
-            tok_push(j).wait_recv()
+        tok_all().wait_recv()
 
     @pl.when(t == tiles - 1)
     def _():
         for q in range(CHIPS):
             for parity, ref in ((0, even), (1, odd)):
-                rows = pl.ds((2 * q + parity) * T, T)
+                rows = pl.ds((CHIPS * parity + q) * T, T)
                 ref[h, q, :, :DH] = (dk_acc[rows, :] * scale).astype(bf16)
                 ref[h, q, :, DH:] = dv_acc[rows, :].astype(bf16)
         swap(h).start()
@@ -422,8 +460,8 @@
         weight_grad(last)
         for hd in range(KVH):
             total_w = dw[hd, zh, x, zl].astype(f32)
+            dw_all(hd).wait_recv()
             for j in range(1, SPREAD):
-                dw_push(hd, j).wait_recv()
                 total_w = total_w + dw_landed[hd, j].astype(f32)
             gw_ref[:, hd*DH:(hd+1)*DH] = total_w[:, :DH]
             gw_ref[:, (KVH+hd)*DH:(KVH+hd+1)*DH] = total_w[:, DH:]
@@ -431,35 +469,20 @@
             for u in range(2):
                 for unit in w_units(hd, u):
                     for phase in range(3):
-                        for k in (1, 2, 3):
-                            w_push(hd, u, unit, phase, k).wait_send()
+                        w_three(hd, u, unit, phase).wait_send()
                     w_swap(hd, u, unit).wait_send()
-            for i in far:
-                @pl.when(chip + i < CHIPS)
-                def _():
-                    for u in range(2):
-                        kv_push(hd, u, i).wait_send()
-
-                @pl.when(i <= chip)
-                def _():
-                    for u in range(2):
-                        kv_forward(hd, u, i).wait_send()
-                    sum_push(hd, i).wait_send()
-
-            @pl.when(core == 0)
-            def _():
-                for u in range(2):
-                    kv_own(hd, u).wait_send()
-
+            for us in (((0,), (1,)) if hd == 0 else ((0, 1),)):
+                wait_for(CHIPS - 1 - chip, lambda count: kv_some(hd, us, count), "wait_send")
+                for k in range(2):
+                    @pl.when(core == k)
+                    def _():
+                        kv_forward(hd, us, k).wait_send()
+            wait_for(chip, lambda count: sum_some(hd, count), "wait_send")
             swap(hd).wait_send()
-            for dy in range(4):
-                gp_forward(hd, dy).wait_send()
-            for dy in (1, 2, 3):
-                gp_push(hd, dy).wait_send()
-            for j in range(1, SPREAD):
-                dw_push(hd, j).wait_send()
-        for j in range(1, GROUP):
-            tok_push(j).wait_send()
+            gp_three(hd).wait_send()
+            gp_forward(hd).wait_send()
+            dw_all(hd).wait_send()
+        tok_all().wait_send()
 
 
 def main(q, do, tokens, weight, cosine, sine):
@@ -484,7 +507,7 @@
         out_shape=[jax.ShapeDtypeStruct(q.shape, bf16), jax.ShapeDtypeStruct(q.shape, bf16),
                    jax.ShapeDtypeStruct((T, features), bf16), jax.ShapeDtypeStruct((rows, width), f32)],
         scratch_shapes=[
-            pltpu.VMEM((KVH, 2, NCTX, T, DH), bf16),
+            pltpu.VMEM((KVH, 2, 2, CHIPS, T, DH), bf16),
             pltpu.VMEM((keys, R), f32), pltpu.VMEM((keys, R), bf16),
             pltpu.VMEM((DH, keys), bf16), pltpu.VMEM((DH, keys), bf16),
             pltpu.VMEM((keys, DH), f32), pltpu.VMEM((keys, DH), f32),
@@ -496,24 +519,51 @@
             pltpu.VMEM((4, 2, 4, 2, 2, rows, T), bf16), pltpu.VMEM((2, 4, 2, rows, GROUP * T), bf16),
             pltpu.VMEM((KVH, 2, 4, 2, rows, 2 * DH), bf16), pltpu.VMEM((KVH, SPREAD, rows, 2 * DH), bf16),
             pltpu.VMEM((T, features), f32),
-            dma((KVH * 36,)), dma((KVH * 36,)), dma((KVH * 4,)), dma((KVH * 4,)), dma,
-            dma((KVH, 2, CHIPS)), dma((KVH, 2, CHIPS)), dma((KVH, 2, CHIPS)), dma((KVH, 2, CHIPS)),
-            dma((KVH,)), dma((KVH,)), dma((KVH, CHIPS)), dma((KVH, CHIPS)),
-            dma((KVH, 4)), dma((KVH, 4)), dma((KVH, 4)), dma((KVH, 4)),
-            dma((KVH, SPREAD)), dma((KVH, SPREAD)), dma((GROUP,)), dma((GROUP,))],
+            dma((30,)), dma((30,)), dma((10,)), dma((10,)), dma,
+            dma((KVH + 1,)), dma((KVH + 1,)), dma((KVH + 1,)), dma((KVH + 1,)),
+            dma((KVH,)), dma((KVH,)), dma((KVH,)), dma((KVH,)),
+            dma((KVH,)), dma((KVH,)), dma((KVH,)), dma((KVH,)),
+            dma((KVH,)), dma((KVH,)), dma, dma],
         compiler_params=pltpu.CompilerParams(
             collective_id=0, has_side_effects=True, vmem_limit_bytes=60 * 2**20),
         name="projection_attention_exchanges",
     )(q, do, tokens, weight, cosine, sine)
 
 
+def copy_kernel(*refs):
+    sems = refs[-1]
+    count = len(refs) // 2
+    copies = []
+    for src, dst in zip(refs[:count], refs[count:-1]):
+        rows = min(32, src.shape[0])
+        for first in range(0, src.shape[0], rows):
+            part = pl.ds(first, rows)
+            copies.append(pltpu.make_async_copy(src.at[part], dst.at[part], sems.at[len(copies)]))
+    for copy in copies:
+        copy.start()
+    for copy in copies:
+        copy.wait()
+
+
+def copy_out(arrays):
+    hbm = pl.BlockSpec(memory_space=pl.ANY)
+    return pl.pallas_call(
+        copy_kernel,
+        in_specs=[hbm] * len(arrays), out_specs=[hbm] * len(arrays),
+        out_shape=[jax.ShapeDtypeStruct(a.shape, a.dtype) for a in arrays],
+        scratch_shapes=[pltpu.SemaphoreType.DMA((16,))],
+        compiler_params=pltpu.CompilerParams(vmem_limit_bytes=60 * 2**20),
+        name="copy_out",
+    )(*arrays)
+
+
 def on_device(inputs, queries, grad_output, kv_weight):
     count = inputs.shape[1]
     ctx = lax.axis_index("ctx")
     cosine, sine = rope_tables(ctx * count + jnp.arange(count, dtype=jnp.int32), DH)
-    attn_out, grad_query, grad_inputs, grad_weight = main(
+    attn_out, grad_query, grad_inputs, grad_weight = copy_out(main(
         queries[0], grad_output[0], inputs[0], kv_weight,
-        jnp.concatenate([cosine, cosine], axis=1), jnp.concatenate([sine, -sine], axis=1))
+        jnp.concatenate([cosine, cosine], axis=1), jnp.concatenate([sine, -sine], axis=1)))
     return (attn_out[None], grad_query[None], grad_inputs[None], grad_weight)
 
 

time: 149 us -> 299 us (2.01)
  Pallas kernels: 140 us -> 298 us
  local copies, waits for them, and re-layouts: 6.88 us -> 0 us
    pallas_call x0 -> x1, Pallas kernels: none -> 164 us  [copy_out(): pl.pallas_call(copy_kernel, in_specs=[hbm] * len(arrays), out_specs=[hbm]...]
    unnamed x10 -> x0, local copies, waits for them, and re-layouts: 6.88 us -> none
    pallas_call x1, Pallas kernels: 140 us -> 133 us  [main(): pl.pallas_call(functools.partial(main_kernel, tiles), grid=(KVH, tiles),...]
where the time goes in v6:
time: 299 us
  Pallas kernels  298 us (100%)
    pallas_call x1, Pallas kernels, copy_out(): pl.pallas_call(copy_kernel, in_specs=[hbm] * len(arrays), out_specs=[hbm]...  164 us
    pallas_call x1, Pallas kernels, main(): pl.pallas_call(functools.partial(main_kernel, tiles), grid=(KVH, tiles),...  133 us

profile of v6, /device:TPU:0, one launch (start us, length us, event | category | flops | bytes accessed | tf_op | source)
XLA Modules:
  0.0 299.2 jit_solution(10541068855215696199)
XLA Ops:
  0.7 0.3 multiply_sine_fusion
  1.0 0.8 pad_maximum_fusion
  1.7 133.5 %projection_attention_exchanges.1 = (bf16[128,8192]{1,0:T(8,128)(2,1)}, bf16[128,8192]{1,0:T(8,128)(2,1)}, bf16[128,4096]{1,0:T(8,128)(2,1)}, f32[32,1024]{1,0:T(8,128)}) custom-call(bf16[128,8192]{1,0:T(8,128)(2,1)} %bitcast.6, bf16[128,8192]{1,0:T(8,128)(2,1)} %bitcast.7, bf16[128,4096]{1,0:T(8,128)(2,1)} %bitcast.8, bf16[32,1024]{1,0:T(8,128)(2,1)} %w_ref.1, ...), custom_call_target="tpu_custom_call" | custom-call | tf_op jit(solution)/shard_map/projection_attention_exchanges/pallas_call | solution.py:500
  135.2 164.0 %copy_out.1 = (bf16[128,8192]{1,0:T(8,128)(2,1)}, bf16[128,8192]{1,0:T(8,128)(2,1)}, bf16[128,4096]{1,0:T(8,128)(2,1)}, f32[32,1024]{1,0:T(8,128)}) custom-call(bf16[128,8192]{1,0:T(8,128)(2,1)} %get-tuple-element.12.refs_0_, bf16[128,8192]{1,0:T(8,128)(2,1)} %get-tuple-element.13.refs_1_, bf16[128,4096]{1,0:T(8,128)(2,1)} %get-tuple-element.14.refs_2_, ...), custom_call_target="tpu_custom_call" | custom-call | tf_op jit(solution)/shard_map/copy_out/pallas_call | solution.py:550
  (2 shorter events, 0.0 us)

commit v7 on v6

--- a/solution.py
+++ b/solution.py
@@ -530,28 +530,32 @@
     )(q, do, tokens, weight, cosine, sine)
 
 
-def copy_kernel(*refs):
-    sems = refs[-1]
-    count = len(refs) // 2
-    copies = []
-    for src, dst in zip(refs[:count], refs[count:-1]):
+def copy_kernel(count, *refs):
+    sources, results, held, load, store = refs[:count], refs[count:2 * count], refs[2 * count:-2], refs[-2], refs[-1]
+    loads, stores = [], []
+    for src, dst, mid in zip(sources, results, held):
         rows = min(32, src.shape[0])
         for first in range(0, src.shape[0], rows):
             part = pl.ds(first, rows)
-            copies.append(pltpu.make_async_copy(src.at[part], dst.at[part], sems.at[len(copies)]))
-    for copy in copies:
+            n = len(loads)
+            loads.append(pltpu.make_async_copy(src.at[part], mid.at[part], load.at[n]))
+            stores.append(pltpu.make_async_copy(mid.at[part], dst.at[part], store.at[n]))
+    for copy in loads:
         copy.start()
-    for copy in copies:
+    for arrived, copy in zip(loads, stores):
+        arrived.wait()
+        copy.start()
+    for copy in stores:
         copy.wait()
 
 
 def copy_out(arrays):
     hbm = pl.BlockSpec(memory_space=pl.ANY)
     return pl.pallas_call(
-        copy_kernel,
+        functools.partial(copy_kernel, len(arrays)),
         in_specs=[hbm] * len(arrays), out_specs=[hbm] * len(arrays),
         out_shape=[jax.ShapeDtypeStruct(a.shape, a.dtype) for a in arrays],
-        scratch_shapes=[pltpu.SemaphoreType.DMA((16,))],
+        scratch_shapes=[pltpu.VMEM(a.shape, a.dtype) for a in arrays] + [pltpu.SemaphoreType.DMA((16,))] * 2,
         compiler_params=pltpu.CompilerParams(vmem_limit_bytes=60 * 2**20),
         name="copy_out",
     )(*arrays)

time: 299 us -> 140 us (0.47)
  Pallas kernels: 298 us -> 138 us
    pallas_call x1, Pallas kernels: 164 us -> 4.79 us  [copy_out(): pl.pallas_call(functools.partial(copy_kernel, len(arrays)), in_specs=[hbm...]
where the time goes in v7:
time: 140 us
  Pallas kernels  138 us (99%)
    pallas_call x1, Pallas kernels, main(): pl.pallas_call(functools.partial(main_kernel, tiles), grid=(KVH, tiles),...  133 us
    pallas_call x1, Pallas kernels, copy_out(): pl.pallas_call(functools.partial(copy_kernel, len(arrays)), in_specs=[hbm...  4.79 us

profile of v7, /device:TPU:0, one launch (start us, length us, event | category | flops | bytes accessed | tf_op | source)
XLA Modules:
  0.0 140.0 jit_solution(2439517084636004164)
XLA Ops:
  0.7 0.3 multiply_sine_fusion
  1.0 0.8 pad_maximum_fusion
  1.7 133.5 %projection_attention_exchanges.1 = (bf16[128,8192]{1,0:T(8,128)(2,1)}, bf16[128,8192]{1,0:T(8,128)(2,1)}, bf16[128,4096]{1,0:T(8,128)(2,1)}, f32[32,1024]{1,0:T(8,128)}) custom-call(bf16[128,8192]{1,0:T(8,128)(2,1)} %bitcast.6, bf16[128,8192]{1,0:T(8,128)(2,1)} %bitcast.7, bf16[128,4096]{1,0:T(8,128)(2,1)} %bitcast.8, bf16[32,1024]{1,0:T(8,128)(2,1)} %w_ref.1, ...), custom_call_target="tpu_custom_call" | custom-call | tf_op jit(solution)/shard_map/projection_attention_exchanges/pallas_call | solution.py:500
  135.2 4.8 %copy_out.1 = (bf16[128,8192]{1,0:T(8,128)(2,1)}, bf16[128,8192]{1,0:T(8,128)(2,1)}, bf16[128,4096]{1,0:T(8,128)(2,1)}, f32[32,1024]{1,0:T(8,128)}) custom-call(bf16[128,8192]{1,0:T(8,128)(2,1)} %get-tuple-element.12.refs_0_, bf16[128,8192]{1,0:T(8,128)(2,1)} %get-tuple-element.13.refs_1_, bf16[128,4096]{1,0:T(8,128)(2,1)} %get-tuple-element.14.refs_2_, ...), custom_call_target="tpu_custom_call" | custom-call | tf_op jit(solution)/shard_map/copy_out/pallas_call | solution.py:554
  (2 shorter events, 0.0 us)

commit v8 on v7

--- a/solution.py
+++ b/solution.py
@@ -202,14 +202,15 @@
         to = lax.rem(z + j % 4, 4)
         return to // 2, lax.rem(x + j // 4, 4), lax.rem(to, 2)
 
-    def dw_push(hd, j):
+    def dw_push(group, j):
         to_zh, to_x, to_zl = across(j)
-        return remote(dw.at[hd, to_zh, to_x, to_zl], dw_landed.at[hd, j], dw_send.at[hd], dw_recv.at[hd],
+        heads = pl.ds(*((0, 2), (2, 1), (3, 1))[group])
+        return remote(dw.at[to_zh, to_x, to_zl, heads], dw_landed.at[j, heads], dw_send.at[group], dw_recv.at[group],
                       device_at(y, to_zh, to_x, to_zl, core))
 
-    def dw_all(hd):
-        region = dw_landed.at[hd, pl.ds(1, SPREAD - 1)]
-        return remote(region, region, dw_send.at[hd], dw_recv.at[hd], partner)
+    def dw_all(group):
+        region = dw_landed.at[pl.ds(1, SPREAD - 1), pl.ds(*((0, 2), (2, 1), (3, 1))[group])]
+        return remote(region, region, dw_send.at[group], dw_recv.at[group], partner)
 
     tok_copy = pltpu.make_async_copy(tok_own.at[y, :, :, :, core], tok_t.at[:, :, :, :, pl.ds(0, T)], tok_local)
 
@@ -260,9 +261,11 @@
         gp_forward(hd).wait_recv()
         part = jnp.dot(tok_t[...].reshape(-1, GROUP * T), gp_all[hd].reshape(GROUP * T, 2 * DH),
                        preferred_element_type=f32)
-        dw[hd] = part.reshape(dw.shape[1:]).astype(bf16)
+        dw[:, :, :, hd] = part.reshape(dw.shape[:3] + dw.shape[4:]).astype(bf16)
+
+    def spread(group):
         for j in range(1, SPREAD):
-            dw_push(hd, j).start()
+            dw_push(group, j).start()
 
     step = h * tiles + t
 
@@ -391,6 +394,10 @@
     def _():
         weight_grad(h - 2)
 
+    @pl.when(step == 2 * KVH - 1)
+    def _():
+        spread(0)
+
     dprobs = lax.dot_general(kv[h, 1].reshape(keys, DH), dos, (((1,), (1,)), ((), ())), preferred_element_type=f32)
     wb = wt_scr[...]
     ds = (dprobs - delta).astype(bf16) * wb
@@ -428,19 +435,19 @@
 
     @pl.when(t == tiles - 1)
     def _():
-        for q in range(CHIPS):
-            for parity, ref in ((0, even), (1, odd)):
+        for parity, ref in ((1, odd), (0, even)):
+            for q in range(CHIPS):
                 rows = pl.ds((CHIPS * parity + q) * T, T)
                 ref[h, q, :, :DH] = (dk_acc[rows, :] * scale).astype(bf16)
                 ref[h, q, :, DH:] = dv_acc[rows, :].astype(bf16)
-        swap(h).start()
+            if parity == 1:
+                swap(h).start()
 
     @pl.when((t == tiles - 1) & (h == KVH - 1))
     def _():
         last = KVH - 1
+        add_pair(last)
         forward_grads(last - 1)
-        add_pair(last)
-        weight_grad(last - 1)
         block = weight.shape[4] * weight.shape[5] * weight.shape[6] * weight.shape[7]
 
         def inputs_part(heads):
@@ -454,15 +461,19 @@
         for columns, part in inputs_part(range(last)):
             gin_acc[:, columns] = part
         finish_block(last)
+        weight_grad(last - 1)
+        spread(1)
         for columns, part in inputs_part([last]):
             gin_ref[:, columns] = (gin_acc[:, columns] + part).astype(bf16)
         forward_grads(last)
         weight_grad(last)
+        spread(2)
         for hd in range(KVH):
-            total_w = dw[hd, zh, x, zl].astype(f32)
-            dw_all(hd).wait_recv()
+            total_w = dw[zh, x, zl, hd].astype(f32)
+            if hd != 1:
+                dw_all(max(hd - 1, 0)).wait_recv()
             for j in range(1, SPREAD):
-                total_w = total_w + dw_landed[hd, j].astype(f32)
+                total_w = total_w + dw_landed[j, hd].astype(f32)
             gw_ref[:, hd*DH:(hd+1)*DH] = total_w[:, :DH]
             gw_ref[:, (KVH+hd)*DH:(KVH+hd+1)*DH] = total_w[:, DH:]
         for hd in range(KVH):
@@ -481,7 +492,8 @@
             swap(hd).wait_send()
             gp_three(hd).wait_send()
             gp_forward(hd).wait_send()
-            dw_all(hd).wait_send()
+            if hd != 1:
+                dw_all(max(hd - 1, 0)).wait_send()
         tok_all().wait_send()
 
 
@@ -517,7 +529,7 @@
             pltpu.VMEM((2 * KVH, T, DH), bf16),
             pltpu.VMEM((KVH, 2, 4, 2, 4, 2, 2, rows, DH), bf16),
             pltpu.VMEM((4, 2, 4, 2, 2, rows, T), bf16), pltpu.VMEM((2, 4, 2, rows, GROUP * T), bf16),
-            pltpu.VMEM((KVH, 2, 4, 2, rows, 2 * DH), bf16), pltpu.VMEM((KVH, SPREAD, rows, 2 * DH), bf16),
+            pltpu.VMEM((2, 4, 2, KVH, rows, 2 * DH), bf16), pltpu.VMEM((SPREAD, KVH, rows, 2 * DH), bf16),
             pltpu.VMEM((T, features), f32),
             dma((30,)), dma((30,)), dma((10,)), dma((10,)), dma,
             dma((KVH + 1,)), dma((KVH + 1,)), dma((KVH + 1,)), dma((KVH + 1,)),

time: 140 us -> 140 us (level)
  no operation moved by 1% of the time
where the time goes in v8:
time: 140 us
  Pallas kernels  138 us (99%)
    pallas_call x1, Pallas kernels, main(): pl.pallas_call(functools.partial(main_kernel, tiles), grid=(KVH, tiles),...  133 us
    pallas_call x1, Pallas kernels, copy_out(): pl.pallas_call(functools.partial(copy_kernel, len(arrays)), in_specs=[hbm...  4.79 us

profile of v8, /device:TPU:0, one launch (start us, length us, event | category | flops | bytes accessed | tf_op | source)
XLA Modules:
  0.0 139.9 jit_solution(2490846178598842875)
XLA Ops:
  0.7 0.3 multiply_sine_fusion
  1.0 0.8 pad_maximum_fusion
  1.7 133.4 %projection_attention_exchanges.1 = (bf16[128,8192]{1,0:T(8,128)(2,1)}, bf16[128,8192]{1,0:T(8,128)(2,1)}, bf16[128,4096]{1,0:T(8,128)(2,1)}, f32[32,1024]{1,0:T(8,128)}) custom-call(bf16[128,8192]{1,0:T(8,128)(2,1)} %bitcast.6, bf16[128,8192]{1,0:T(8,128)(2,1)} %bitcast.7, bf16[128,4096]{1,0:T(8,128)(2,1)} %bitcast.8, bf16[32,1024]{1,0:T(8,128)(2,1)} %w_ref.1, ...), custom_call_target="tpu_custom_call" | custom-call | tf_op jit(solution)/shard_map/projection_attention_exchanges/pallas_call | solution.py:512
  135.1 4.8 %copy_out.1 = (bf16[128,8192]{1,0:T(8,128)(2,1)}, bf16[128,8192]{1,0:T(8,128)(2,1)}, bf16[128,4096]{1,0:T(8,128)(2,1)}, f32[32,1024]{1,0:T(8,128)}) custom-call(bf16[128,8192]{1,0:T(8,128)(2,1)} %get-tuple-element.12.refs_0_, bf16[128,8192]{1,0:T(8,128)(2,1)} %get-tuple-element.13.refs_1_, bf16[128,4096]{1,0:T(8,128)(2,1)} %get-tuple-element.14.refs_2_, ...), custom_call_target="tpu_custom_call" | custom-call | tf_op jit(solution)/shard_map/copy_out/pallas_call | solution.py:566
  (2 shorter events, 0.0 us)
